TPU v7x, 512 devices: a whole 4x8x8 slice. The times are simulated.
512 devices in a mesh: section: 32 (over z_hi, y), dp: 16 (over z_lo, x, core).
Axes of the slice: x: 4, y: 8, z: 8 (z_hi: 4, z_lo: 2; z = z_hi * 2 + z_lo), core: 2. Of those that a mesh axis runs over, the one named last changes fastest.
Arguments:
- saved_input: bfloat16 [32, 2048, 12288], P('section', 'dp'), may hold values from -6 to 6
- norm_gain: float32 [32, 12288], P('section'), may hold values from 0.25 to 1.75
- left_in: bfloat16 [32, 2048, 64], P('section', 'dp'), may hold values from -6 to 6
- right_in: bfloat16 [32, 12288, 64], P('section', 'dp'), may hold values from -0.75 to 0.75
- basis: bfloat16 [32, 12288, 64], P('section', 'dp'), may hold values from -0.0546875 to 0.0546875
Outputs:
- gain_grad: float32 [32, 12288], P('section', 'dp')
- bias_grad: float32 [32, 12288], P('section', 'dp')
- left_out: bfloat16 [32, 2048, 64], P('section', 'dp')
- right_out: bfloat16 [32, 12288, 64], P('section', 'dp')
All inputs are finite; a program needn't handle non-finite values.
Results may differ from a plain program's by a relative error of at most 0.02.
Values may be sent and summed in bfloat16 or wider, within the bound.
No kernel may reach another device: no remote copies, remote signals or barrier semaphores. Data moves between devices by JAX's collectives and lax.ppermute only.
A program may use at most 64 MiB of HBM per device.

v0:
```python
import jax
import jax.numpy as jnp
from jax import lax
from jax.sharding import PartitionSpec as P


def shifted(x, axis, by):
    size = lax.axis_size(axis)
    pairs = [(i, i + by) for i in range(size) if 0 <= i + by < size]
    return lax.ppermute(x, axis, pairs)


def replica_sums(terms):
    totals = lax.psum(terms.astype(jnp.bfloat16), "dp").astype(jnp.float32)
    width = terms.shape[1] // lax.axis_size("dp")
    return lax.dynamic_slice_in_dim(totals, lax.axis_index("dp") * width, width, 1)


def on_device(saved_input, norm_gain, left_in, right_in, basis):
    left = left_in[0]
    rebuilt = jnp.dot(
        left,
        lax.all_gather(right_in, "dp", axis=1, tiled=True)[0].T,
        preferred_element_type=jnp.float32,
    )
    values = saved_input[0].astype(jnp.float32)
    center = values - jnp.mean(values, axis=1, keepdims=True)
    inverse = lax.rsqrt(jnp.mean(center * center, axis=1, keepdims=True) + 1e-05)
    normed = center * inverse
    tokens_all = saved_input.shape[1] * lax.axis_size("dp")
    factor = 1.0 / jnp.sqrt(jnp.float32(tokens_all))
    terms = jnp.stack([jnp.sum(rebuilt * normed, axis=0), jnp.sum(rebuilt, axis=0)]) * factor
    scaled = rebuilt * norm_gain[0][None, :]
    first = jnp.mean(scaled, axis=1, keepdims=True)
    second = jnp.mean(scaled * normed, axis=1, keepdims=True)
    boundary = (inverse * (scaled - first - normed * second)).astype(jnp.bfloat16)
    columns = boundary
    power = jnp.dot(
        columns,
        lax.all_gather(basis, "dp", axis=1, tiled=True)[0],
        preferred_element_type=jnp.float32,
    )
    gram_local = jnp.dot(power.T, power, precision=lax.Precision.HIGHEST)
    gram = lax.psum(gram_local, "dp")
    lower = jnp.linalg.cholesky(gram)
    ortho = jax.scipy.linalg.solve_triangular(lower, power.T, lower=True).T.astype(jnp.bfloat16)
    columns = boundary
    feature_share = lax.psum_scatter(
        jnp.dot(columns.T, ortho, preferred_element_type=jnp.float32).astype(jnp.bfloat16),
        "dp",
        scatter_dimension=0,
        tiled=True,
    )
    shares = replica_sums(terms)
    moved_left, moved_right = shifted((ortho, feature_share), "section", -1)
    return (shares[0][None], shares[1][None], moved_left[None], moved_right[None])


def solution(mesh):
    placed = (
        P("section", "dp", None),
        P("section", None),
        P("section", "dp", None),
        P("section", "dp", None),
        P("section", "dp", None),
    )
    return jax.shard_map(
        on_device,
        mesh=mesh,
        in_specs=placed,
        out_specs=(
            P("section", "dp"),
            P("section", "dp"),
            P("section", "dp", None),
            P("section", "dp", None),
        ),
        check_vma=False,
    )
```

profile of v0, /device:TPU:56, one launch (start us, length us, event | category | flops | bytes accessed | tf_op | source)
XLA Modules:
  0.0 250.8 jit_solution(14119464149567248667)
XLA Ops:
  7.2 0.0 copy-start
  7.2 0.0 copy-start.1
  7.2 0.0 copy-start.3
  7.2 0.0 all-gather.3.cloned.1.call-start
  7.2 0.7 all-gather.3.cloned.1.call-update
  7.9 0.0 all-gather.5.cloned.1.call-start
  8.0 0.7 all-gather.5.cloned.1.call-update
  8.7 0.0 reduce-scatter.2.cloned.1.call-start
  8.7 2.4 convert_reduce_fusion
  11.1 2.9 %fusion.11 = f32[128]{0:T(128)S(1)} fusion(bf16[1,128,12288]{2,1,0:T(8,128)(2,1)} %param.5, f32[128]{0:T(128)S(1)} %broadcast_multiply_fusion.2), kind=kLoop, calls=%fused_computation.14 | loop fusion | flops 6291328 | bytes 3146752 | tf_op jit(solution)/shard_map/reduce_sum | solution.py:28
  14.0 38.8 %all-gather.3.cloned.1.call-done = bf16[1,12288,64]{1,2,0:T(8,128)(2,1)} async-done(((bf16[1,768,64]{1,2,0:T(8,128)(2,1)}), bf16[1,12288,64]{1,2,0:T(8,128)(2,1)}) %all-gather.3.cloned.1.call-update) | async-done | bytes 1572880 | tf_op jit(solution)/shard_map/all_gather | solution.py:23
  52.9 0.0 copy-done
  52.9 0.0 copy-done.1
  52.9 0.0 copy-done.3
  52.9 4.1 %fusion.7 = (f32[128]{0:T(128)S(1)}, f32[12288]{0:T(1024)S(1)}, f32[128]{0:T(128)S(1)}, f32[12288]{0:T(1024)S(1)}, f32[128,12288]{1,0:T(8,128)S(1)}) fusion(bf16[1,128,12288]{2,1,0:T(8,128)(2,1)S(1)} %copy-done.1, f32[12288]{0:T(1024)S(1)} %bitcast.60, f32[128]{0:T(128)S(1)} %add_rsqrt_fusion, f32[128]{0:T(128)S(1)} %broadcast_multiply_fusion.2, ...), kind=kOutput, calls=%fused_computation.10 | convolution fusion | flops 217030400 | bytes 11175936 | tf_op jit(solution)/shard_map/dot_general | solution.py:21
  57.0 3.0 %fusion.10 = bf16[128,12288]{1,0:T(8,128)(2,1)} fusion(bf16[1,128,12288]{2,1,0:T(8,128)(2,1)S(1)} %copy-done.1, f32[128,12288]{1,0:T(8,128)S(1)} %get-tuple-element.10, f32[128]{0:T(128)S(1)} %get-tuple-element.11, f32[128]{0:T(128)S(1)} %get-tuple-element.12, f32[12288]{0:T(1024)S(1)} %bitcast.61, f32[128]{0:T(128)S(1)} %add_rsqrt_fusion, ...), kind=kLoop, calls=%fused_computation.13 | loop fusion | flops 14155776 | bytes 12634112 | tf_op jit(solution)/shard_map/convert_element_type | solution.py:36
  60.1 0.0 copy-start.2
  60.1 33.5 %all-gather.5.cloned.1.call-done = bf16[1,12288,64]{1,2,0:T(8,128)(2,1)} async-done(((bf16[1,768,64]{1,2,0:T(8,128)(2,1)}), bf16[1,12288,64]{1,2,0:T(8,128)(2,1)}) %all-gather.5.cloned.1.call-update) | async-done | bytes 1572880 | tf_op jit(solution)/shard_map/all_gather | solution.py:40
  93.6 3.6 %fusion.12 = f32[128,64]{0,1:T(8,128)S(1)} fusion(bf16[128,12288]{1,0:T(8,128)(2,1)} %fusion.10, bf16[1,12288,64]{1,2,0:T(8,128)(2,1)} %all-gather.5.cloned.1.call-done), kind=kOutput, calls=%fused_computation.16 | convolution fusion | flops 201326592 | bytes 4751360 | tf_op jit(solution)/shard_map/dot_general | solution.py:38
  97.1 0.2 fusion.22
  97.3 54.7 %psum.15 = f32[64,64]{0,1:T(8,128)S(1)} all-reduce(f32[64,64]{0,1:T(8,128)S(1)} %fusion.22), channel_id=1, replica_groups=mesh['section'=32,'dp'=16] {'dp'}, use_global_device_ids=true, to_apply=%region_7.8 | all-reduce | flops 4096 | bytes 32768 | tf_op jit(solution)/shard_map/psum | solution.py:44
  152.0 0.1 copy.10
  152.1 5.8 %cholesky.16 = f32[64,64]{1,0:T(8,128)S(1)} custom-call(f32[64,64]{1,0:T(8,128)S(1)} %fusion.19), custom_call_target="Cholesky" | custom-call | tf_op jit(solution)/shard_map/jit(cholesky)/cholesky | solution.py:45
  158.0 0.6 compare_reduce_fusion
  158.6 0.7 fusion.17
  159.3 4.9 %custom-call.7 = f32[1,64,64]{1,2,0:T(8,128)S(1)} custom-call(f32[1,64,64]{2,1,0:T(8,128)S(1)} %fusion.17), custom_call_target="InvertDiagBlocksLowerTriangular" | custom-call | tf_op jit(solution)/shard_map/jit(_solve_triangular)/triangular_solve | solution.py:46
  164.2 0.3 convolution_convert_fusion.1
  164.5 0.0 copy-done.2
  164.5 1.7 convolution_convert_fusion
  166.2 0.0 reduce-scatter.2.cloned.1.call-update
  166.2 3.4 %collective-permute-start = (bf16[128,64]{0,1:T(8,128)(2,1)S(1)}, bf16[128,64]{0,1:T(8,128)(2,1)S(1)}, u32[]{:S(2)}, u32[]{:S(2)}) collective-permute-start(bf16[128,64]{0,1:T(8,128)(2,1)S(1)} %convolution_convert_fusion.1), channel_id=1, source_target_pairs={{16,0},{32,16},{48,32},{64,48},{80,64},{96,80},{112,96},{128,112},... | collective-permute-start | bytes 49160 | tf_op jit(solution)/shard_map/ppermute | solution.py:10
  169.6 0.1 fusion.16
  169.7 53.1 %psum.14 = bf16[2,12288]{1,0:T(2,128)(2,1)S(1)} all-reduce(bf16[2,12288]{1,0:T(2,128)(2,1)S(1)} %fusion.16), channel_id=1, replica_groups=mesh['section'=32,'dp'=16] {'dp'}, use_global_device_ids=true, to_apply=%region_4.0 | all-reduce | flops 24576 | bytes 98304 | tf_op jit(solution)/shard_map/psum | solution.py:14
  222.8 9.8 %reduce-scatter.2.cloned.1.call-done = bf16[768,64]{0,1:T(8,128)(2,1)} async-done(((bf16[12288,64]{0,1:T(8,128)(2,1)}), bf16[768,64]{0,1:T(8,128)(2,1)}) %reduce-scatter.2.cloned.1.call-update) | async-done | bytes 98320 | tf_op jit(solution)/shard_map/reduce_scatter | solution.py:48
  232.6 3.2 %collective-permute-start.1 = (bf16[768,64]{0,1:T(8,128)(2,1)}, bf16[768,64]{0,1:T(8,128)(2,1)S(1)}, u32[]{:S(2)}, u32[]{:S(2)}) collective-permute-start(bf16[768,64]{0,1:T(8,128)(2,1)} %reduce-scatter.2.cloned.1.call-done), channel_id=1, source_target_pairs={{16,0},{32,16},{48,32},{64,48},{80,64},{96,80},{112,96},{128,112},... | collective-permute-start | bytes 294920 | tf_op jit(solution)/shard_map/ppermute | solution.py:10
  235.8 0.6 fusion.21
  236.4 0.0 collective-permute-done
  236.4 6.7 %collective-permute-done.1 = bf16[768,64]{0,1:T(8,128)(2,1)S(1)} collective-permute-done((bf16[768,64]{0,1:T(8,128)(2,1)}, bf16[768,64]{0,1:T(8,128)(2,1)S(1)}, u32[]{:S(2)}, u32[]{:S(2)}) %collective-permute-start.1) | collective-permute-done | bytes 98336 | tf_op jit(solution)/shard_map/ppermute | solution.py:10
  243.1 0.6 copy.14
  243.7 0.6 copy.15
  (6 shorter events, 0.1 us)
Async XLA Ops:
  7.2 45.7 %copy-start = (bf16[1,128,64]{1,2,0:T(8,128)(2,1)S(1)}, bf16[1,128,64]{1,2,0:T(8,128)(2,1)}, u32[]{:S(2)}) copy-start(bf16[1,128,64]{1,2,0:T(8,128)(2,1)} %param.7) | copy-start | bytes 49156
  7.2 45.7 %copy-start.1 = (bf16[1,128,12288]{2,1,0:T(8,128)(2,1)S(1)}, bf16[1,128,12288]{2,1,0:T(8,128)(2,1)}, u32[]{:S(2)}) copy-start(bf16[1,128,12288]{2,1,0:T(8,128)(2,1)} %param.5) | copy-start | bytes 9437188
  7.2 45.7 %copy-start.3 = (f32[1,12288]{1,0:T(1,128)S(1)}, f32[1,12288]{1,0:T(1,128)}, u32[]{:S(2)}) copy-start(f32[1,12288]{1,0:T(1,128)} %param.6) | copy-start | bytes 147460
  7.2 45.7 %all-gather.3.cloned.1.call-start = ((), (), s32[]{:S(2)}) async-start(), calls=%async_computation.1 | async-start | bytes 1671168 | tf_op jit(solution)/shard_map/all_gather | solution.py:23
  7.9 85.6 %all-gather.5.cloned.1.call-start = ((), (), s32[]{:S(2)}) async-start(), calls=%async_computation.2 | async-start | bytes 1671168 | tf_op jit(solution)/shard_map/all_gather | solution.py:40
  8.7 223.9 %reduce-scatter.2.cloned.1.call-start = ((), (), s32[]{:S(2)}) async-start(), calls=%async_computation.3 | async-start | bytes 1671168 | tf_op jit(solution)/shard_map/reduce_scatter | solution.py:48
  60.1 104.4 %copy-start.2 = (bf16[128,12288]{1,0:T(8,128)(2,1)S(1)}, bf16[128,12288]{1,0:T(8,128)(2,1)}, u32[]{:S(2)}) copy-start(bf16[128,12288]{1,0:T(8,128)(2,1)} %fusion.10) | copy-start | bytes 9437188
  166.2 70.2 %collective-permute-start = (bf16[128,64]{0,1:T(8,128)(2,1)S(1)}, bf16[128,64]{0,1:T(8,128)(2,1)S(1)}, u32[]{:S(2)}, u32[]{:S(2)}) collective-permute-start(bf16[128,64]{0,1:T(8,128)(2,1)S(1)} %convolution_convert_fusion.1), channel_id=1, source_target_pairs={{16,0},{32,16},{48,32},{64,48},{80,64},{96,80},{112,96},{128,112},... | collective-permute-start | bytes 49160 | tf_op jit(solution)/shard_map/ppermute | solution.py:10
  232.6 10.5 %collective-permute-start.1 = (bf16[768,64]{0,1:T(8,128)(2,1)}, bf16[768,64]{0,1:T(8,128)(2,1)S(1)}, u32[]{:S(2)}, u32[]{:S(2)}) collective-permute-start(bf16[768,64]{0,1:T(8,128)(2,1)} %reduce-scatter.2.cloned.1.call-done), channel_id=1, source_target_pairs={{16,0},{32,16},{48,32},{64,48},{80,64},{96,80},{112,96},{128,112},... | collective-permute-start | bytes 294920 | tf_op jit(solution)/shard_map/ppermute | solution.py:10
Sparse Core Ops, SparseCore 0:
  10.1 42.6 all-gather.2
  55.0 38.5 all-gather.4
  166.3 66.1 reduce-scatter.1
where the time goes:
time: 251 us
  blocking collectives  108 us (43%)
  waiting for transfers between devices  90.2 us (36%)
  other arithmetic  20.5 us (8%)
  between operations  13.9 us (6%)
  matrix products  9.86 us (4%)
  starting transfers between devices  6.69 us (3%)
    psum x1, blocking collectives, on_device(): gram = lax.psum(gram_local, 'dp')  54.7 us
    psum x1, blocking collectives, replica_sums(): totals = lax.psum(terms.astype(jnp.bfloat16), 'dp').astype(jnp.float32)  53.1 us
    all_gather x1, waiting for transfers between devices, on_device(): lax.all_gather(right_in, 'dp', axis=1, tiled=True)[0]  38.8 us
    all_gather x1, waiting for transfers between devices, on_device(): lax.all_gather(basis, 'dp', axis=1, tiled=True)[0]  33.5 us
    reduce_scatter x1, waiting for transfers between devices, on_device(): lax.psum_scatter(jnp.dot(columns.T, ortho, preferred_element_type=jnp.flo...  9.81 us
    ppermute x2, waiting for transfers between devices, shifted(): return lax.ppermute(x, axis, pairs)  6.66 us
    ppermute x2, starting transfers between devices, shifted(): return lax.ppermute(x, axis, pairs)  6.58 us
    another operation x3, other arithmetic, on_device(): lower = jnp.linalg.cholesky(gram)  6.52 us
  transfers between devices with their start and end apart: 5, of which 4 were waited for; matrix products, arithmetic and copies ran while one was open for 5% of the time, Pallas kernels for 0%

commit v1 on v0

v1 whole, which is shorter than its diff:
```python
import jax
import jax.numpy as jnp
from jax import lax
from jax.experimental import pallas as pl
from jax.experimental.pallas import tpu as pltpu
from jax.sharding import PartitionSpec as P

LANES = 128
F32 = jnp.float32
BF16 = jnp.bfloat16
NT = (((1,), (1,)), ((), ()))


def main_kernel(parity, x, gain, left_t, full, keep, send, power_t, rebuilt, boundary, rows, tail):
    blocks, _, width = full.shape
    tokens = x.shape[0]
    features = blocks * width
    rank = power_t.shape[0]
    chunks = width // LANES
    zero = jnp.zeros((tokens, LANES), F32)

    def columns(j, c):
        return pl.ds(pl.multiple_of(j * width + c * LANES, LANES), LANES)

    def row_mean(total):
        return jnp.broadcast_to(jnp.sum(total, axis=1, keepdims=True) * (1.0 / features), total.shape)

    def add(j, total):
        for c in range(chunks):
            total = total + x[:, columns(j, c)].astype(F32)
        return total

    rows[0] = row_mean(lax.fori_loop(0, blocks, add, zero))

    def add_squares(j, total):
        for c in range(chunks):
            center = x[:, columns(j, c)].astype(F32) - rows[0]
            total = total + center * center
        return total

    rows[1] = lax.rsqrt(row_mean(lax.fori_loop(0, blocks, add_squares, zero)) + 1e-05)

    left = left_t[...].astype(F32).T.astype(BF16)

    rows[2] = zero
    rows[3] = zero
    for side, out in enumerate((keep, send)):
        own = parity[0] ^ side

        @pl.loop(0, blocks // 2)
        def _(k):
            j = 2 * k + own
            rebuilt[j] = jnp.dot(left, full[j, :rank, :], preferred_element_type=F32)
            first, second = rows[2], rows[3]
            for c in range(chunks):
                lanes = slice(c * LANES, (c + 1) * LANES)
                part = rebuilt[j, :, lanes]
                normed = (x[:, columns(j, c)].astype(F32) - rows[0]) * rows[1]
                scaled = part * gain[:, columns(j, c)]
                first = first + scaled
                second = second + scaled * normed
                out[k, rank : rank + 1, lanes] = jnp.sum(part * normed, axis=0, keepdims=True)
                out[k, rank + 1 : rank + 2, lanes] = jnp.sum(part, axis=0, keepdims=True)
            rows[2] = first
            rows[3] = second

    rows[2] = row_mean(rows[2])
    rows[3] = row_mean(rows[3])

    def project(j, total):
        for c in range(chunks):
            lanes = slice(c * LANES, (c + 1) * LANES)
            normed = (x[:, columns(j, c)].astype(F32) - rows[0]) * rows[1]
            scaled = rebuilt[j, :, lanes] * gain[:, columns(j, c)]
            boundary[j, :, lanes] = (rows[1] * (scaled - rows[2] - normed * rows[3])).astype(BF16)
        return total + lax.dot_general(full[j, rank:, :], boundary[j], NT, preferred_element_type=F32)

    power = lax.fori_loop(0, blocks, project, jnp.zeros((rank, tokens), F32))
    power_t[...] = power
    gram = lax.dot_general(power, power, NT, precision=lax.Precision.HIGHEST, preferred_element_type=F32)
    half = rank // 2
    tail[...] = jnp.zeros_like(tail)
    packed = jnp.concatenate([gram[:half], gram[half:]], axis=1)
    for q in range(half):
        tail[q // chunks : q // chunks + 1, (q % chunks) * LANES : (q % chunks + 1) * LANES] = packed[q : q + 1]
    high = power.astype(BF16)
    low = (power - high.astype(F32)).astype(BF16)
    both = jnp.concatenate([high, low], axis=0)

    for side, out in enumerate((keep, send)):
        own = parity[0] ^ side

        @pl.loop(0, blocks // 2)
        def _(k):
            terms = jnp.dot(both, boundary[2 * k + own], preferred_element_type=F32)
            out[k, :rank, :] = terms[:rank] + terms[rank:]
            out[k, rank + 2 :, :] = tail[: out.shape[1] - rank - 2]


def inverse_factor(gram):
    size = gram.shape[0]
    wide = 2 * size
    row = lax.broadcasted_iota(jnp.int32, (size, size), 0)
    col = lax.broadcasted_iota(jnp.int32, (size, size), 1)
    eye = jnp.where(row == col, 1.0, 0.0).astype(F32)
    work = jnp.concatenate([gram, eye], axis=1)
    parts = [work[8 * i : 8 * i + 8] for i in range(size // 8)]
    below = lax.broadcasted_iota(jnp.int32, (8, wide), 0)
    for k in range(size):
        at, r = divmod(k, 8)
        pivot = jnp.broadcast_to(parts[at][r : r + 1], (8, wide))
        scale = 1.0 / jnp.broadcast_to(pivot[:, k : k + 1], (8, wide))
        pivot = pivot * scale
        for i in range(at, size // 8):
            step = jnp.broadcast_to(parts[i][:, k : k + 1], (8, wide)) * pivot
            if i == at:
                step = jnp.where(below > r, step, 0.0)
            parts[i] = parts[i] - step
    work = jnp.concatenate(parts, axis=0)
    diagonal = jnp.sum(jnp.where(row == col, work[:, :size], 0.0), axis=1, keepdims=True)
    return work[:, size:] * lax.rsqrt(diagonal)


def post_kernel(factor, terms, power_t, gain_out, bias_out, moved, square):
    rank, tokens = power_t.shape
    width = terms.shape[2]
    chunks = width // LANES
    half = rank // 2
    total = terms[0]
    for j in range(1, terms.shape[0]):
        total = total + terms[j]
    gain_out[...] = total[rank : rank + 1] * factor
    bias_out[...] = total[rank + 1 : rank + 2] * factor
    for q in range(half):
        line = rank + 2 + q // chunks
        start = (q % chunks) * LANES
        square[q : q + 1, :] = total[line : line + 1, start : start + LANES]
    packed = square[...]
    inverse = inverse_factor(jnp.concatenate([packed[:, :rank], packed[:, rank:]], axis=0))
    exact = dict(precision=lax.Precision.HIGHEST, preferred_element_type=F32)
    moved[:, :width] = jnp.dot(inverse, total[:rank], **exact).astype(BF16)
    moved[:, width:] = jnp.dot(inverse, power_t[...], **exact).astype(BF16)


def on_device(saved_input, norm_gain, left_in, right_in, basis):
    _, tokens, features = saved_input.shape
    width, rank = right_in.shape[1:]
    replicas = lax.axis_size("dp")
    pairs = replicas // 2
    chunks = width // LANES
    height = rank + 2 + -(-(rank // 2) // chunks)
    vmem = pl.BlockSpec(memory_space=pltpu.VMEM)
    smem = pl.BlockSpec(memory_space=pltpu.SMEM)

    own = jnp.concatenate([right_in[0].T, basis[0].T], axis=0)
    full = lax.all_gather(own, "dp")
    parity = (lax.axis_index("dp") % 2).astype(jnp.int32).reshape(1)
    block = jax.ShapeDtypeStruct((pairs, height, width), F32)
    keep, send, power_t = pl.pallas_call(
        main_kernel,
        out_shape=(block, block, jax.ShapeDtypeStruct((rank, tokens), F32)),
        in_specs=[smem, vmem, vmem, vmem, vmem],
        out_specs=(vmem, vmem, vmem),
        scratch_shapes=[
            pltpu.VMEM((replicas, tokens, width), F32),
            pltpu.VMEM((replicas, tokens, width), BF16),
            pltpu.VMEM((4, tokens, LANES), F32),
            pltpu.VMEM((8, width), F32),
        ],
        compiler_params=pltpu.CompilerParams(vmem_limit_bytes=40 * 2**20),
    )(parity, saved_input[0], norm_gain, left_in[0].T, full)
    other = lax.ppermute(send, "dp", [(i, i ^ 1) for i in range(replicas)])
    groups = [[2 * k + c for k in range(pairs)] for c in range(2)]
    terms = lax.all_to_all(keep + other, "dp", 0, 0, tiled=True, axis_index_groups=groups)

    factor = float(1.0 / (tokens * replicas) ** 0.5)
    gain_grad, bias_grad, moved = pl.pallas_call(
        lambda *refs: post_kernel(factor, *refs),
        out_shape=(
            jax.ShapeDtypeStruct((1, width), F32),
            jax.ShapeDtypeStruct((1, width), F32),
            jax.ShapeDtypeStruct((rank, width + tokens), BF16),
        ),
        in_specs=[vmem, vmem],
        out_specs=(vmem, vmem, vmem),
        scratch_shapes=[pltpu.VMEM((rank // 2, LANES), F32)],
        compiler_params=pltpu.CompilerParams(vmem_limit_bytes=16 * 2**20),
    )(terms, power_t)
    sections = lax.axis_size("section")
    moved = lax.ppermute(moved, "section", [(i, i - 1) for i in range(1, sections)])
    return gain_grad, bias_grad, moved[:, width:].T[None], moved[:, :width].T[None]


def solution(mesh):
    placed = (
        P("section", "dp", None),
        P("section", None),
        P("section", "dp", None),
        P("section", "dp", None),
        P("section", "dp", None),
    )
    return jax.shard_map(
        on_device,
        mesh=mesh,
        in_specs=placed,
        out_specs=(
            P("section", "dp"),
            P("section", "dp"),
            P("section", "dp", None),
            P("section", "dp", None),
        ),
        check_vma=False,
    )
```

time: 251 us -> 137 us (0.55)
  blocking collectives: 108 us -> 27.7 us
  waiting for transfers between devices: 90.2 us -> 57.4 us
  Pallas kernels: 0 us -> 23.9 us
  other arithmetic: 20.5 us -> 1.87 us
  matrix products: 9.86 us -> 0 us
  local copies, waits for them, and re-layouts: 1.93 us -> 6.55 us
    psum x2 -> x0, blocking collectives: 108 us -> none  [the longest x1 54.7 us: on_device(): gram = lax.psum(gram_local, 'dp')]
    all_to_all x0 -> x1, blocking collectives: none -> 27.7 us  [on_device(): lax.all_to_all(keep + other, 'dp', 0, 0, tiled=True, axis_index_groups=gr...]
    all_gather x2 -> x1, waiting for transfers between devices: 72.3 us -> 46.5 us  [on_device(): full = lax.all_gather(own, 'dp')]
    pallas_call x0 -> x2, Pallas kernels: none -> 23.9 us  [the longest x1 14.6 us: on_device(): pl.pallas_call(main_kernel, out_shape=(block, block, jax.ShapeDtypeStruct...]
    another operation x5 -> x0, other arithmetic: 12.1 us -> none  [the longest x3 6.52 us: on_device(): lower = jnp.linalg.cholesky(gram)]
    reduce_scatter x1 -> x0, waiting for transfers between devices: 9.81 us -> none  [on_device(): lax.psum_scatter(jnp.dot(columns.T, ortho, preferred_element_type=jnp.flo...]
    dot_general x4 -> x0, matrix products: 9.61 us -> none  [the longest x1 4.15 us: on_device(): jnp.dot(left, lax.all_gather(right_in, 'dp', axis=1, tiled=True)[0].T, pr...]
    reduce_sum x2 -> x0, other arithmetic: 5.26 us -> none  [the longest x1 2.88 us: on_device(): jnp.mean(center * center, axis=1, keepdims=True) + 1e-05]
  transfers between devices with their start and end apart: 5 -> 3, of which waited for: 4 -> 3; matrix products, arithmetic and copies ran while one was open for 5% -> 0% of each run, Pallas kernels for 0% -> 0%
where the time goes in v1:
time: 137 us
  waiting for transfers between devices  57.4 us (42%)
  blocking collectives  27.7 us (20%)
  Pallas kernels  23.9 us (17%)
  between operations  14.1 us (10%)
  local copies, waits for them, and re-layouts  6.55 us (5%)
  starting transfers between devices  5.52 us (4%)
  other arithmetic  1.87 us (1%)
    all_gather x1, waiting for transfers between devices, on_device(): full = lax.all_gather(own, 'dp')  46.5 us
    all_to_all x1, blocking collectives, on_device(): lax.all_to_all(keep + other, 'dp', 0, 0, tiled=True, axis_index_groups=gr...  27.7 us
    pallas_call x1, Pallas kernels, on_device(): pl.pallas_call(main_kernel, out_shape=(block, block, jax.ShapeDtypeStruct...  14.6 us
    pallas_call x1, Pallas kernels, on_device(): pl.pallas_call(lambda *refs: post_kernel(factor, *refs), out_shape=(jax.S...  9.29 us
    ppermute x1, waiting for transfers between devices, on_device(): lax.ppermute(moved, 'section', [(i, i - 1) for i in range(1, sections)])  7.4 us
    unnamed x8, local copies, waits for them, and re-layouts  5.29 us
    ppermute x1, waiting for transfers between devices, on_device(): other = lax.ppermute(send, 'dp', [(i, i ^ 1) for i in range(replicas)])  3.44 us
    ppermute x1, starting transfers between devices, on_device(): lax.ppermute(moved, 'section', [(i, i - 1) for i in range(1, sections)])  3.34 us
  transfers between devices with their start and end apart: 3, of which 3 were waited for; matrix products, arithmetic and copies ran while one was open for 0% of the time, Pallas kernels for 0%

profile of v1, /device:TPU:56, one launch (start us, length us, event | category | flops | bytes accessed | tf_op | source)
XLA Modules:
  0.0 137.0 jit_solution(2886545029239501521)
XLA Ops:
  7.2 0.0 all-gather.3.cloned.1.call-start
  7.2 1.6 %pad_maximum_fusion = bf16[128,768]{1,0:T(8,128)(2,1)} fusion(bf16[64,768]{1,0:T(8,128)(2,1)} %bitcast.23, bf16[64,768]{1,0:T(8,128)(2,1)} %bitcast.24), kind=kLoop, calls=%fused_computation | loop fusion | flops 393216 | bytes 393216 | tf_op jit(solution)/shard_map/concatenate | solution.py:155
  8.8 0.0 all-gather.3.cloned.1.call-update
  8.9 46.5 %all-gather.3.cloned.1.call-done = bf16[2048,768]{1,0:T(8,128)(2,1)} async-done(((bf16[128,768]{1,0:T(8,128)(2,1)}), bf16[2048,768]{1,0:T(8,128)(2,1)}) %all-gather.3.cloned.1.call-update) | async-done | bytes 3145744 | tf_op jit(solution)/shard_map/all_gather | solution.py:156
  55.4 0.0 copy-start
  55.4 1.9 %copy-done = bf16[1,128,12288]{2,1,0:T(8,128)(2,1)S(1)} copy-done((bf16[1,128,12288]{2,1,0:T(8,128)(2,1)S(1)}, bf16[1,128,12288]{2,1,0:T(8,128)(2,1)}, u32[]{:S(2)}) %copy-start) | copy-done | bytes 3145752
  57.3 0.0 copy-start.1
  57.3 1.9 %copy-done.1 = bf16[2048,768]{1,0:T(8,128)(2,1)S(1)} copy-done((bf16[2048,768]{1,0:T(8,128)(2,1)S(1)}, bf16[2048,768]{1,0:T(8,128)(2,1)}, u32[]{:S(2)}) %copy-start.1) | copy-done | bytes 3145752
  59.2 0.0 copy-start.2
  59.2 0.8 copy-done.2
  60.0 0.0 copy-start.3
  60.0 0.7 copy-done.3
  60.7 14.6 %shard_map.84 = (f32[8,72,768]{2,1,0:T(8,128)S(1)}, f32[8,72,768]{2,1,0:T(8,128)S(1)}, f32[64,128]{1,0:T(8,128)S(1)}) custom-call(s32[1]{0:T(128)} %bitcast.parity, bf16[128,12288]{1,0:T(8,128)(2,1)S(1)} %bitcast.20, f32[1,12288]{1,0:T(1,128)S(1)} %copy-done.2, bf16[64,128]{1,0:T(8,128)(2,1)S(1)} %bitcast.22, bf16[16,128,768]{2,1,0:T(8,128)(2,1)S(1)} %bitcast.21), custom_call_target="tpu_custom_call" | custom-call | tf_op jit(solution)/shard_map/pallas_call | solution.py:159
  75.3 2.1 %collective-permute-start = (f32[8,72,768]{2,1,0:T(8,128)S(1)}, f32[8,72,768]{2,1,0:T(8,128)S(1)}, u32[]{:S(2)}, u32[]{:S(2)}) collective-permute-start(f32[8,72,768]{2,1,0:T(8,128)S(1)} %get-tuple-element.11), channel_id=1, source_target_pairs={{0,1},{1,0},{2,3},{3,2},{4,5},{5,4},{6,7},{7,6},{8,9},{9,8},{10,11... | collective-permute-start | bytes 5308424 | tf_op jit(solution)/shard_map/ppermute | solution.py:172
  77.5 3.4 %collective-permute-done = f32[8,72,768]{2,1,0:T(8,128)S(1)} collective-permute-done((f32[8,72,768]{2,1,0:T(8,128)S(1)}, f32[8,72,768]{2,1,0:T(8,128)S(1)}, u32[]{:S(2)}, u32[]{:S(2)}) %collective-permute-start) | collective-permute-done | bytes 1769504 | tf_op jit(solution)/shard_map/ppermute | solution.py:172
  80.9 0.2 add.8
  81.2 27.7 %all_to_all.5.refs_0_ = f32[8,72,768]{2,1,0:T(8,128)S(1)} all-to-all(f32[8,72,768]{2,1,0:T(8,128)S(1)} %add.8), channel_id=1, replica_groups={{0,2,4,6,8,10,12,14},{1,3,5,7,9,11,13,15},{16,18,20,22,24,26,28,30},{17..., dimensions={0} | all-to-all | bytes 3538944 | tf_op jit(solution)/shard_map/all_to_all | solution.py:174
  108.9 9.3 %shard_map.85 = (f32[1,768]{1,0:T(1,128)}, f32[1,768]{1,0:T(1,128)}, bf16[64,896]{1,0:T(8,128)(2,1)S(1)}) custom-call(f32[8,72,768]{2,1,0:T(8,128)S(1)} %all_to_all.5.refs_0_, f32[64,128]{1,0:T(8,128)S(1)} %get-tuple-element.12.refs_1_), custom_call_target="tpu_custom_call" | custom-call | tf_op jit(solution)/shard_map/pallas_call | solution.py:177
  118.2 3.3 %collective-permute-start.1 = (bf16[64,896]{1,0:T(8,128)(2,1)S(1)}, bf16[64,896]{1,0:T(8,128)(2,1)S(1)}, u32[]{:S(2)}, u32[]{:S(2)}) collective-permute-start(bf16[64,896]{1,0:T(8,128)(2,1)S(1)} %get-tuple-element.15), channel_id=1, source_target_pairs={{16,0},{32,16},{48,32},{64,48},{80,64},{96,80},{112,96},{128,112},... | collective-permute-start | bytes 344072 | tf_op jit(solution)/shard_map/ppermute | solution.py:190
  121.5 7.4 %collective-permute-done.1 = bf16[64,896]{1,0:T(8,128)(2,1)S(1)} collective-permute-done((bf16[64,896]{1,0:T(8,128)(2,1)S(1)}, bf16[64,896]{1,0:T(8,128)(2,1)S(1)}, u32[]{:S(2)}, u32[]{:S(2)}) %collective-permute-start.1) | collective-permute-done | bytes 114720 | tf_op jit(solution)/shard_map/ppermute | solution.py:190
  128.9 0.6 slice_bitcast_fusion.1
  129.5 0.6 slice_bitcast_fusion
Async XLA Ops:
  7.2 48.2 %all-gather.3.cloned.1.call-start = ((), (), s32[]{:S(2)}) async-start(), calls=%async_computation.1 | async-start | bytes 3342336 | tf_op jit(solution)/shard_map/all_gather | solution.py:156
  55.4 1.9 %copy-start = (bf16[1,128,12288]{2,1,0:T(8,128)(2,1)S(1)}, bf16[1,128,12288]{2,1,0:T(8,128)(2,1)}, u32[]{:S(2)}) copy-start(bf16[1,128,12288]{2,1,0:T(8,128)(2,1)} %param.5) | copy-start | bytes 9437188
  57.3 1.9 %copy-start.1 = (bf16[2048,768]{1,0:T(8,128)(2,1)S(1)}, bf16[2048,768]{1,0:T(8,128)(2,1)}, u32[]{:S(2)}) copy-start(bf16[2048,768]{1,0:T(8,128)(2,1)} %all-gather.3.cloned.1.call-done) | copy-start | bytes 9437188
  59.2 0.8 copy-start.2
  60.0 0.7 copy-start.3
  75.3 5.6 %collective-permute-start = (f32[8,72,768]{2,1,0:T(8,128)S(1)}, f32[8,72,768]{2,1,0:T(8,128)S(1)}, u32[]{:S(2)}, u32[]{:S(2)}) collective-permute-start(f32[8,72,768]{2,1,0:T(8,128)S(1)} %get-tuple-element.11), channel_id=1, source_target_pairs={{0,1},{1,0},{2,3},{3,2},{4,5},{5,4},{6,7},{7,6},{8,9},{9,8},{10,11... | collective-permute-start | bytes 5308424 | tf_op jit(solution)/shard_map/ppermute | solution.py:172
  118.2 10.7 %collective-permute-start.1 = (bf16[64,896]{1,0:T(8,128)(2,1)S(1)}, bf16[64,896]{1,0:T(8,128)(2,1)S(1)}, u32[]{:S(2)}, u32[]{:S(2)}) collective-permute-start(bf16[64,896]{1,0:T(8,128)(2,1)S(1)} %get-tuple-element.15), channel_id=1, source_target_pairs={{16,0},{32,16},{48,32},{64,48},{80,64},{96,80},{112,96},{128,112},... | collective-permute-start | bytes 344072 | tf_op jit(solution)/shard_map/ppermute | solution.py:190
Sparse Core Ops, SparseCore 0:
  10.1 45.1 all-gather.2

commit v2 on v0

v2 whole, which is shorter than its diff:
```python
import jax
import jax.numpy as jnp
from jax import lax
from jax.experimental import pallas as pl
from jax.experimental.pallas import tpu as pltpu
from jax.sharding import PartitionSpec as P

LANES = 128
GROUP = 16
F32 = jnp.float32
BF16 = jnp.bfloat16
NT = (((1,), (1,)), ((), ()))
VMEM = pl.BlockSpec(memory_space=pltpu.VMEM)
SMEM = pl.BlockSpec(memory_space=pltpu.SMEM)


def fold(value):
    return value[:8] + value[8:]


def gain_pass(j, k, left, factors, x, gain, rows, rebuilt, sums):
    tokens, width = rebuilt.shape[1:]
    rank = left.shape[1]
    rebuilt[k] = jnp.dot(left, factors[k, :rank, :], preferred_element_type=F32)
    chunks = range(width // LANES)
    columns = [pl.ds(pl.multiple_of(j * width + c * LANES, LANES), LANES) for c in chunks]
    gains = [jnp.broadcast_to(gain[:, columns[c]], (GROUP, LANES)) for c in chunks]
    products = [jnp.zeros((8, LANES), F32) for _ in chunks]
    plain = [jnp.zeros((8, LANES), F32) for _ in chunks]
    for r in range(0, tokens, GROUP):
        group = slice(r, r + GROUP)
        mean, inverse = rows[0, group], rows[1, group]
        first, second = rows[2, group], rows[3, group]
        for c in chunks:
            part = rebuilt[k, group, c * LANES : (c + 1) * LANES]
            normed = (x[group, columns[c]].astype(F32) - mean) * inverse
            scaled = part * gains[c]
            first = first + scaled
            second = second + scaled * normed
            products[c] = products[c] + fold(part * normed)
            plain[c] = plain[c] + fold(part)
        rows[2, group] = first
        rows[3, group] = second
    for c in chunks:
        lanes = slice(c * LANES, (c + 1) * LANES)
        sums[k, 0:1, lanes] = jnp.sum(products[c], axis=0, keepdims=True)
        sums[k, 1:2, lanes] = jnp.sum(plain[c], axis=0, keepdims=True)


def row_mean(total, features):
    return jnp.broadcast_to(jnp.sum(total, axis=1, keepdims=True) * (1.0 / features), total.shape)


def first_kernel(parity, x_hbm, gain, left_t, mine, x, left_out, rows, rebuilt, sums, arrived):
    half, _, width = mine.shape
    tokens, features = x.shape
    blocks = 2 * half
    chunks = range(width // LANES)

    def fetch(j):
        columns = pl.ds(pl.multiple_of(j * width, LANES), width)
        return pltpu.make_async_copy(x_hbm.at[:, columns], x.at[:, columns], arrived.at[j])

    @pl.loop(0, blocks)
    def _(j):
        fetch(j).start()

    left_out[...] = left_t[...].astype(F32).T.astype(BF16)
    left = left_out[...]
    rows[...] = jnp.zeros_like(rows)

    @pl.loop(0, blocks)
    def _(j):
        fetch(j).wait()
        for r in range(0, tokens, GROUP):
            group = slice(r, r + GROUP)
            total = rows[0, group]
            for c in chunks:
                columns = pl.ds(pl.multiple_of(j * width + c * LANES, LANES), LANES)
                total = total + x[group, columns].astype(F32)
            rows[0, group] = total

    rows[0] = row_mean(rows[0], features)

    @pl.loop(0, blocks)
    def _(j):
        for r in range(0, tokens, GROUP):
            group = slice(r, r + GROUP)
            total, mean = rows[1, group], rows[0, group]
            for c in chunks:
                columns = pl.ds(pl.multiple_of(j * width + c * LANES, LANES), LANES)
                center = x[group, columns].astype(F32) - mean
                total = total + center * center
            rows[1, group] = total

    rows[1] = lax.rsqrt(row_mean(rows[1], features) + 1e-05)

    @pl.loop(0, half)
    def _(k):
        gain_pass(2 * k + parity[0], k, left, mine, x, gain, rows, rebuilt, sums)


def second_kernel(
    parity, x, gain, left_ref, rows_in, rebuilt_mine, mine, theirs, power_t, both_out, kept, tail, send, rows, rebuilt, sums, moved
):
    half, height, width = theirs.shape
    tokens, features = x.shape
    rank = left_ref.shape[1]
    chunks = range(width // LANES)
    left = left_ref[...]
    rows[...] = rows_in[...]

    @pl.loop(0, half)
    def _(k):
        gain_pass(2 * k + (1 - parity[0]), k, left, theirs, x, gain, rows, rebuilt, sums)

    first = row_mean(rows[2], features)
    second = row_mean(rows[3], features)
    rows[2] = rows[1] * rows[1] * second
    rows[3] = rows[0] * rows[2] - rows[1] * first

    def project(side, factors, source, target):
        def step(k, total):
            j = 2 * k + (parity[0] ^ side)
            columns = [pl.ds(pl.multiple_of(j * width + c * LANES, LANES), LANES) for c in chunks]
            gains = [jnp.broadcast_to(gain[:, columns[c]], (GROUP, LANES)) for c in chunks]
            for r in range(0, tokens, GROUP):
                group = slice(r, r + GROUP)
                inverse, slope, offset = rows[1, group], rows[2, group], rows[3, group]
                for c in chunks:
                    lanes = slice(c * LANES, (c + 1) * LANES)
                    scaled = source[k, group, lanes] * gains[c]
                    value = scaled * inverse - x[group, columns[c]].astype(F32) * slope + offset
                    target[k, group, lanes] = value.astype(BF16)
            return total + lax.dot_general(factors[k, rank:, :], target[k], NT, preferred_element_type=F32)

        return step

    power = lax.fori_loop(0, half, project(0, mine, rebuilt_mine, kept), jnp.zeros((rank, tokens), F32))
    power = lax.fori_loop(0, half, project(1, theirs, rebuilt, moved), power)
    power_t[...] = power
    gram = lax.dot_general(power, power, NT, precision=lax.Precision.HIGHEST, preferred_element_type=F32)
    side = rank // 2
    tail[...] = jnp.zeros_like(tail)
    packed = jnp.concatenate([gram[:side], gram[side:]], axis=1)
    per = width // LANES
    for q in range(side):
        tail[q // per : q // per + 1, (q % per) * LANES : (q % per + 1) * LANES] = packed[q : q + 1]
    high = power.astype(BF16)
    low = (power - high.astype(F32)).astype(BF16)
    both = jnp.concatenate([high, low], axis=0)
    both_out[...] = both
    feature_terms(both, moved, sums, tail, send)


def feature_terms(both, boundary, sums, tail, out):
    half, height, _ = out.shape
    rank = both.shape[0] // 2

    @pl.loop(0, half)
    def _(k):
        terms = jnp.dot(both, boundary[k], preferred_element_type=F32)
        out[k, :rank, :] = terms[:rank] + terms[rank:]
        out[k, rank : rank + 2, :] = sums[k, 0:2, :]
        out[k, rank + 2 :, :] = tail[: height - rank - 2]


def third_kernel(both, kept, sums, tail, keep):
    feature_terms(both[...], kept, sums, tail, keep)


def inverse_factor(gram):
    size = gram.shape[0]
    wide = 2 * size
    count = size // 8
    row = lax.broadcasted_iota(jnp.int32, (size, size), 0)
    col = lax.broadcasted_iota(jnp.int32, (size, size), 1)
    work = jnp.concatenate([gram, jnp.where(row == col, 1.0, 0.0).astype(F32)], axis=1)
    parts = [work[8 * i : 8 * i + 8] for i in range(count)]
    done = []
    for b in range(count):
        lines = [parts[b][r : r + 1] for r in range(8)]
        entry = {
            (i, j): jnp.broadcast_to(lines[i][:, 8 * b + j : 8 * b + j + 1], (1, wide))
            for i in range(8)
            for j in range(i + 1)
        }
        ratio, scale = {}, []
        for r in range(8):
            scale.append(1.0 / entry[r, r])
            for i in range(r + 1, 8):
                ratio[i, r] = entry[i, r] * scale[r]
            for i in range(r + 1, 8):
                for j in range(r + 1, i + 1):
                    entry[i, j] = entry[i, j] - ratio[i, r] * entry[j, r]
                lines[i] = lines[i] - ratio[i, r] * lines[r]
        done += [lines[r] * lax.rsqrt(entry[r, r]) for r in range(8)]
        solved = [None] * 8
        for r in reversed(range(8)):
            solved[r] = lines[r] * scale[r]
            for j in range(r + 1, 8):
                solved[r] = solved[r] - ratio[j, r] * solved[j]
        for i in range(b + 1, count):
            value = parts[i]
            for r in range(8):
                value = value - jnp.broadcast_to(parts[i][:, 8 * b + r : 8 * b + r + 1], (8, wide)) * solved[r]
            parts[i] = value
    return jnp.concatenate(done, axis=0)[:, size:]


def post_kernel(factor, terms, power_t, gain_out, bias_out, moved, square):
    rank, tokens = power_t.shape
    width = terms.shape[2]
    chunks = width // LANES
    half = rank // 2
    total = terms[0]
    for j in range(1, terms.shape[0]):
        total = total + terms[j]
    gain_out[...] = total[rank : rank + 1] * factor
    bias_out[...] = total[rank + 1 : rank + 2] * factor
    for q in range(half):
        line = rank + 2 + q // chunks
        start = (q % chunks) * LANES
        square[q : q + 1, :] = total[line : line + 1, start : start + LANES]
    packed = square[...]
    inverse = inverse_factor(jnp.concatenate([packed[:, :rank], packed[:, rank:]], axis=0))
    exact = dict(precision=lax.Precision.HIGHEST, preferred_element_type=F32)
    moved[:, :width] = jnp.dot(inverse, total[:rank], **exact).astype(BF16)
    moved[:, width:] = jnp.dot(inverse, power_t[...], **exact).astype(BF16)


def limit(mib):
    return pltpu.CompilerParams(vmem_limit_bytes=mib * 2**20)


def cost(mib):
    return pl.CostEstimate(flops=0, bytes_accessed=mib * 2**20, transcendentals=0)


def on_device(saved_input, norm_gain, left_in, right_in, basis):
    _, tokens, features = saved_input.shape
    width, rank = right_in.shape[1:]
    replicas = lax.axis_size("dp")
    half = replicas // 2
    chunks = width // LANES
    height = rank + 2 + -(-(rank // 2) // chunks)
    others = [(i, i ^ 1) for i in range(replicas)]
    groups = [[2 * k + c for k in range(half)] for c in range(2)]
    shape = jax.ShapeDtypeStruct

    own = jnp.concatenate([right_in[0].T, basis[0].T], axis=0)
    copies = jnp.broadcast_to(own[None], (half,) + own.shape)
    mine = lax.all_to_all(copies, "dp", 0, 0, tiled=True, axis_index_groups=groups)
    theirs = lax.ppermute(mine, "dp", others)
    parity = (lax.axis_index("dp") & 1).astype(jnp.int32).reshape(1)
    x, left, rows, rebuilt, sums = pl.pallas_call(
        first_kernel,
        out_shape=(
            shape((tokens, features), BF16),
            shape((tokens, rank), BF16),
            shape((4, tokens, LANES), F32),
            shape((half, tokens, width), F32),
            shape((half, 8, width), F32),
        ),
        in_specs=[SMEM, pl.BlockSpec(memory_space=pltpu.HBM), VMEM, VMEM, VMEM],
        out_specs=(VMEM,) * 5,
        scratch_shapes=[pltpu.SemaphoreType.DMA((replicas,))],
        compiler_params=limit(20),
        cost_estimate=cost(24),
    )(parity, saved_input[0], norm_gain, left_in[0].T, mine)
    power_t, both, kept, tail, send = pl.pallas_call(
        second_kernel,
        out_shape=(
            shape((rank, tokens), F32),
            shape((2 * rank, tokens), BF16),
            shape((half, tokens, width), BF16),
            shape((8, width), F32),
            shape((half, height, width), F32),
        ),
        in_specs=[SMEM] + [VMEM] * 7,
        out_specs=(VMEM,) * 5,
        scratch_shapes=[
            pltpu.VMEM((4, tokens, LANES), F32),
            pltpu.VMEM((half, tokens, width), F32),
            pltpu.VMEM((half, 8, width), F32),
            pltpu.VMEM((half, tokens, width), BF16),
        ],
        compiler_params=limit(32),
    )(parity, x, norm_gain, left, rows, rebuilt, mine, theirs)
    other = lax.ppermute(send, "dp", others)
    keep = pl.pallas_call(
        third_kernel,
        out_shape=shape((half, height, width), F32),
        in_specs=[VMEM] * 4,
        out_specs=VMEM,
        compiler_params=limit(12),
        cost_estimate=cost(12),
    )(both, kept, sums, tail)
    terms = lax.all_to_all(keep + other, "dp", 0, 0, tiled=True, axis_index_groups=groups)

    factor = float(1.0 / (tokens * replicas) ** 0.5)
    gain_grad, bias_grad, moved = pl.pallas_call(
        lambda *refs: post_kernel(factor, *refs),
        out_shape=(shape((1, width), F32), shape((1, width), F32), shape((rank, width + tokens), BF16)),
        in_specs=[VMEM, VMEM],
        out_specs=(VMEM,) * 3,
        scratch_shapes=[pltpu.VMEM((rank // 2, LANES), F32)],
        compiler_params=limit(16),
    )(terms, power_t)
    sections = lax.axis_size("section")
    moved = lax.ppermute(moved, "section", [(i, i - 1) for i in range(1, sections)])
    return gain_grad, bias_grad, moved[:, width:].T[None], moved[:, :width].T[None]


def solution(mesh):
    placed = (
        P("section", "dp", None),
        P("section", None),
        P("section", "dp", None),
        P("section", "dp", None),
        P("section", "dp", None),
    )
    return jax.shard_map(
        on_device,
        mesh=mesh,
        in_specs=placed,
        out_specs=(
            P("section", "dp"),
            P("section", "dp"),
            P("section", "dp", None),
            P("section", "dp", None),
        ),
        check_vma=False,
    )
```

time: 251 us -> 95.8 us (0.38)
  waiting for transfers between devices: 90.2 us -> 9.44 us
  blocking collectives: 108 us -> 54.1 us
  other arithmetic: 20.5 us -> 1.19 us
  Pallas kernels: 0 us -> 18 us
  between operations: 13.9 us -> 0.73 us
  matrix products: 9.86 us -> 0 us
    psum x2 -> x0, blocking collectives: 108 us -> none  [the longest x1 54.7 us: on_device(): gram = lax.psum(gram_local, 'dp')]
    all_gather x2 -> x0, waiting for transfers between devices: 72.3 us -> none  [the longest x1 38.8 us: on_device(): lax.all_gather(right_in, 'dp', axis=1, tiled=True)[0]]
    all_to_all x0 -> x2, blocking collectives: none -> 54.1 us  [the longest x1 27.5 us: on_device(): lax.all_to_all(copies, 'dp', 0, 0, tiled=True, axis_index_groups=groups)]
    pallas_call x0 -> x4, Pallas kernels: none -> 18 us  [the longest x1 8.46 us: on_device(): pl.pallas_call(second_kernel, out_shape=(shape((rank, tokens), F32), shap...]
    another operation x5 -> x0, other arithmetic: 12.1 us -> none  [the longest x3 6.52 us: on_device(): lower = jnp.linalg.cholesky(gram)]
    reduce_scatter x1 -> x0, waiting for transfers between devices: 9.81 us -> none  [on_device(): lax.psum_scatter(jnp.dot(columns.T, ortho, preferred_element_type=jnp.flo...]
    dot_general x4 -> x0, matrix products: 9.61 us -> none  [the longest x1 4.15 us: on_device(): jnp.dot(left, lax.all_gather(right_in, 'dp', axis=1, tiled=True)[0].T, pr...]
    reduce_sum x2 -> x0, other arithmetic: 5.26 us -> none  [the longest x1 2.88 us: on_device(): jnp.mean(center * center, axis=1, keepdims=True) + 1e-05]
  transfers between devices with their start and end apart: 5 -> 3, of which waited for: 4 -> 2; matrix products, arithmetic and copies ran while one was open for 5% -> 0% of each run, Pallas kernels for 0% -> 7%
where the time goes in v2:
time: 95.8 us; the launch traced here: 94.3 us
  blocking collectives  54.1 us (56%)
  Pallas kernels  18 us (19%)
  waiting for transfers between devices  9.44 us (10%)
  starting transfers between devices  7.6 us (8%)
  local copies, waits for them, and re-layouts  3.25 us (3%)
  other arithmetic  1.19 us (1%)
    all_to_all x1, blocking collectives, on_device(): lax.all_to_all(copies, 'dp', 0, 0, tiled=True, axis_index_groups=groups)  27.5 us
    all_to_all x1, blocking collectives, on_device(): lax.all_to_all(keep + other, 'dp', 0, 0, tiled=True, axis_index_groups=gr...  26.6 us
    pallas_call x1, Pallas kernels, on_device(): pl.pallas_call(second_kernel, out_shape=(shape((rank, tokens), F32), shap...  8.46 us
    ppermute x1, waiting for transfers between devices, on_device(): lax.ppermute(moved, 'section', [(i, i - 1) for i in range(1, sections)])  7.71 us
    pallas_call x1, Pallas kernels, on_device(): pl.pallas_call(first_kernel, out_shape=(shape((tokens, features), BF16),...  5.06 us
    ppermute x1, starting transfers between devices, on_device(): lax.ppermute(moved, 'section', [(i, i - 1) for i in range(1, sections)])  3.25 us
    pallas_call x1, Pallas kernels, on_device(): pl.pallas_call(lambda *refs: post_kernel(factor, *refs), out_shape=(shape...  2.92 us
    ppermute x1, starting transfers between devices, on_device(): other = lax.ppermute(send, 'dp', others)  2.44 us
  transfers between devices with their start and end apart: 3, of which 2 were waited for; matrix products, arithmetic and copies ran while one was open for 0% of the time, Pallas kernels for 7%

profile of v2, /device:TPU:56, one launch (start us, length us, event | category | flops | bytes accessed | tf_op | source)
XLA Modules:
  0.0 94.3 jit_solution(10560415293282348514)
XLA Ops:
  0.6 1.0 %pad_maximum_fusion = bf16[128,768]{1,0:T(8,128)(2,1)S(1)} fusion(bf16[64,768]{1,0:T(8,128)(2,1)} %bitcast.21, bf16[64,768]{1,0:T(8,128)(2,1)} %bitcast.22), kind=kLoop, calls=%fused_computation | loop fusion | flops 393216 | bytes 393216 | tf_op jit(solution)/shard_map/concatenate | solution.py:251
  1.6 0.1 broadcast_in_dim.12
  1.7 0.0 copy-start.1
  1.7 0.0 copy-start.2
  1.7 27.5 %all_to_all.10.mine = bf16[8,128,768]{2,1,0:T(8,128)(2,1)S(1)} all-to-all(bf16[8,128,768]{2,1,0:T(8,128)(2,1)S(1)} %broadcast_in_dim.12), channel_id=1, replica_groups={{0,2,4,6,8,10,12,14},{1,3,5,7,9,11,13,15},{16,18,20,22,24,26,28,30},{17..., dimensions={0} | all-to-all | bytes 3145728 | tf_op jit(solution)/shard_map/all_to_all | solution.py:253
  29.2 1.9 %collective-permute-start = (bf16[8,128,768]{2,1,0:T(8,128)(2,1)S(1)}, bf16[8,128,768]{2,1,0:T(8,128)(2,1)S(1)}, u32[]{:S(2)}, u32[]{:S(2)}) collective-permute-start(bf16[8,128,768]{2,1,0:T(8,128)(2,1)S(1)} %all_to_all.10.mine), channel_id=1, source_target_pairs={{0,1},{1,0},{2,3},{3,2},{4,5},{5,4},{6,7},{7,6},{8,9},{9,8},{10,11... | collective-permute-start | bytes 4718600 | tf_op jit(solution)/shard_map/ppermute | solution.py:254
  31.2 0.0 copy-done.1
  31.2 0.0 copy-done.2
  31.2 0.0 copy-start
  31.2 1.9 %copy-done = bf16[1,128,12288]{2,1,0:T(8,128)(2,1)S(1)} copy-done((bf16[1,128,12288]{2,1,0:T(8,128)(2,1)S(1)}, bf16[1,128,12288]{2,1,0:T(8,128)(2,1)}, u32[]{:S(2)}) %copy-start) | copy-done | bytes 3145752
  33.1 5.1 %shard_map.84 = (bf16[128,12288]{1,0:T(8,128)(2,1)S(1)}, bf16[128,64]{1,0:T(8,128)(2,1)S(1)}, f32[4,128,128]{2,1,0:T(8,128)S(1)}, f32[8,128,768]{2,1,0:T(8,128)S(1)}, f32[8,8,768]{2,1,0:T(8,128)S(1)}) custom-call(s32[1]{0:T(128)} %bitcast.parity, bf16[128,12288]{1,0:T(8,128)(2,1)S(1)} %bitcast.19, f32[1,12288]{1,0:T(1,128)S(1)} %copy-done.1, ...), custom_call_target="tpu_custom_call" | custom-call | bytes 25165824 | tf_op jit(solution)/shard_map/pallas_call | solution.py:256
  38.1 0.0 collective-permute-done.theirs
  38.2 8.5 %shard_map.85 = (f32[64,128]{1,0:T(8,128)S(1)}, bf16[128,128]{1,0:T(8,128)(2,1)S(1)}, bf16[8,128,768]{2,1,0:T(8,128)(2,1)S(1)}, f32[8,768]{1,0:T(8,128)S(1)}, f32[8,72,768]{2,1,0:T(8,128)S(1)}) custom-call(s32[1]{0:T(128)} %bitcast.parity, bf16[128,12288]{1,0:T(8,128)(2,1)S(1)} %get-tuple-element.17.x, f32[1,12288]{1,0:T(1,128)S(1)} %copy-done.1, ...), custom_call_target="tpu_custom_call" | custom-call | tf_op jit(solution)/shard_map/pallas_call | solution.py:271
  46.6 2.4 %collective-permute-start.1 = (f32[8,72,768]{2,1,0:T(8,128)S(1)}, f32[8,72,768]{2,1,0:T(8,128)S(1)}, u32[]{:S(2)}, u32[]{:S(2)}) collective-permute-start(f32[8,72,768]{2,1,0:T(8,128)S(1)} %get-tuple-element.25), channel_id=1, source_target_pairs={{0,1},{1,0},{2,3},{3,2},{4,5},{5,4},{6,7},{7,6},{8,9},{9,8},{10,11... | collective-permute-start | bytes 5308424 | tf_op jit(solution)/shard_map/ppermute | solution.py:290
  49.1 1.6 %shard_map.86 = f32[8,72,768]{2,1,0:T(8,128)S(1)} custom-call(bf16[128,128]{1,0:T(8,128)(2,1)S(1)} %get-tuple-element.21.both, bf16[8,128,768]{2,1,0:T(8,128)(2,1)S(1)} %get-tuple-element.22.kept, f32[8,8,768]{2,1,0:T(8,128)S(1)} %get-tuple-element.23.sums, f32[8,768]{1,0:T(8,128)S(1)} %get-tuple-element.24.tail), custom_call_target="tpu_custom_call" | custom-call | bytes 12582912 | tf_op jit(solution)/shard_map/pallas_call | solution.py:291
  50.6 1.7 %collective-permute-done.1 = f32[8,72,768]{2,1,0:T(8,128)S(1)} collective-permute-done((f32[8,72,768]{2,1,0:T(8,128)S(1)}, f32[8,72,768]{2,1,0:T(8,128)S(1)}, u32[]{:S(2)}, u32[]{:S(2)}) %collective-permute-start.1) | collective-permute-done | bytes 1769504 | tf_op jit(solution)/shard_map/ppermute | solution.py:290
  52.4 0.2 add.3
  52.6 26.6 %all_to_all.11.refs_0_ = f32[8,72,768]{2,1,0:T(8,128)S(1)} all-to-all(f32[8,72,768]{2,1,0:T(8,128)S(1)} %add.3), channel_id=1, replica_groups={{0,2,4,6,8,10,12,14},{1,3,5,7,9,11,13,15},{16,18,20,22,24,26,28,30},{17..., dimensions={0} | all-to-all | bytes 3538944 | tf_op jit(solution)/shard_map/all_to_all | solution.py:299
  79.2 2.9 %shard_map.87 = (f32[1,768]{1,0:T(1,128)}, f32[1,768]{1,0:T(1,128)}, bf16[64,896]{1,0:T(8,128)(2,1)S(1)}) custom-call(f32[8,72,768]{2,1,0:T(8,128)S(1)} %all_to_all.11.refs_0_, f32[64,128]{1,0:T(8,128)S(1)} %get-tuple-element.26.refs_1_), custom_call_target="tpu_custom_call" | custom-call | tf_op jit(solution)/shard_map/pallas_call | solution.py:302
  82.1 3.2 %collective-permute-start.2 = (bf16[64,896]{1,0:T(8,128)(2,1)S(1)}, bf16[64,896]{1,0:T(8,128)(2,1)S(1)}, u32[]{:S(2)}, u32[]{:S(2)}) collective-permute-start(bf16[64,896]{1,0:T(8,128)(2,1)S(1)} %get-tuple-element.29), channel_id=1, source_target_pairs={{16,0},{32,16},{48,32},{64,48},{80,64},{96,80},{112,96},{128,112},... | collective-permute-start | bytes 344072 | tf_op jit(solution)/shard_map/ppermute | solution.py:311
  85.3 7.7 %collective-permute-done.2 = bf16[64,896]{1,0:T(8,128)(2,1)S(1)} collective-permute-done((bf16[64,896]{1,0:T(8,128)(2,1)S(1)}, bf16[64,896]{1,0:T(8,128)(2,1)S(1)}, u32[]{:S(2)}, u32[]{:S(2)}) %collective-permute-start.2) | collective-permute-done | bytes 114720 | tf_op jit(solution)/shard_map/ppermute | solution.py:311
  93.0 0.6 slice_bitcast_fusion.1
  93.7 0.6 slice_bitcast_fusion
Async XLA Ops:
  1.7 29.5 %copy-start.1 = (f32[1,12288]{1,0:T(1,128)S(1)}, f32[1,12288]{1,0:T(1,128)}, u32[]{:S(2)}) copy-start(f32[1,12288]{1,0:T(1,128)} %gain.3) | copy-start | bytes 147460
  1.7 29.5 %copy-start.2 = (bf16[1,128,64]{1,2,0:T(8,128)(2,1)S(1)}, bf16[1,128,64]{1,2,0:T(8,128)(2,1)}, u32[]{:S(2)}) copy-start(bf16[1,128,64]{1,2,0:T(8,128)(2,1)} %param.7) | copy-start | bytes 49156
  29.2 8.9 %collective-permute-start = (bf16[8,128,768]{2,1,0:T(8,128)(2,1)S(1)}, bf16[8,128,768]{2,1,0:T(8,128)(2,1)S(1)}, u32[]{:S(2)}, u32[]{:S(2)}) collective-permute-start(bf16[8,128,768]{2,1,0:T(8,128)(2,1)S(1)} %all_to_all.10.mine), channel_id=1, source_target_pairs={{0,1},{1,0},{2,3},{3,2},{4,5},{5,4},{6,7},{7,6},{8,9},{9,8},{10,11... | collective-permute-start | bytes 4718600 | tf_op jit(solution)/shard_map/ppermute | solution.py:254
  31.2 1.9 %copy-start = (bf16[1,128,12288]{2,1,0:T(8,128)(2,1)S(1)}, bf16[1,128,12288]{2,1,0:T(8,128)(2,1)}, u32[]{:S(2)}) copy-start(bf16[1,128,12288]{2,1,0:T(8,128)(2,1)} %param.5) | copy-start | bytes 9437188
  46.6 5.7 %collective-permute-start.1 = (f32[8,72,768]{2,1,0:T(8,128)S(1)}, f32[8,72,768]{2,1,0:T(8,128)S(1)}, u32[]{:S(2)}, u32[]{:S(2)}) collective-permute-start(f32[8,72,768]{2,1,0:T(8,128)S(1)} %get-tuple-element.25), channel_id=1, source_target_pairs={{0,1},{1,0},{2,3},{3,2},{4,5},{5,4},{6,7},{7,6},{8,9},{9,8},{10,11... | collective-permute-start | bytes 5308424 | tf_op jit(solution)/shard_map/ppermute | solution.py:290
  82.1 11.0 %collective-permute-start.2 = (bf16[64,896]{1,0:T(8,128)(2,1)S(1)}, bf16[64,896]{1,0:T(8,128)(2,1)S(1)}, u32[]{:S(2)}, u32[]{:S(2)}) collective-permute-start(bf16[64,896]{1,0:T(8,128)(2,1)S(1)} %get-tuple-element.29), channel_id=1, source_target_pairs={{16,0},{32,16},{48,32},{64,48},{80,64},{96,80},{112,96},{128,112},... | collective-permute-start | bytes 344072 | tf_op jit(solution)/shard_map/ppermute | solution.py:311

commit v3 on v2

--- a/solution.py
+++ b/solution.py
@@ -7,6 +7,7 @@
 
 LANES = 128
 GROUP = 16
+UNROLL = 4
 F32 = jnp.float32
 BF16 = jnp.bfloat16
 NT = (((1,), (1,)), ((), ()))
@@ -18,33 +19,42 @@
     return value[:8] + value[8:]
 
 
-def gain_pass(j, k, left, factors, x, gain, rows, rebuilt, sums):
+def gain_pass(j, k, left, factors, x, gain, rows, rebuilt, sums, plain=True, normal=True):
     tokens, width = rebuilt.shape[1:]
     rank = left.shape[1]
-    rebuilt[k] = jnp.dot(left, factors[k, :rank, :], preferred_element_type=F32)
     chunks = range(width // LANES)
     columns = [pl.ds(pl.multiple_of(j * width + c * LANES, LANES), LANES) for c in chunks]
     gains = [jnp.broadcast_to(gain[:, columns[c]], (GROUP, LANES)) for c in chunks]
     products = [jnp.zeros((8, LANES), F32) for _ in chunks]
-    plain = [jnp.zeros((8, LANES), F32) for _ in chunks]
+    bare = [jnp.zeros((8, LANES), F32) for _ in chunks]
+    if plain:
+        rebuilt[k] = jnp.dot(left, factors[k, :rank, :], preferred_element_type=F32)
     for r in range(0, tokens, GROUP):
         group = slice(r, r + GROUP)
-        mean, inverse = rows[0, group], rows[1, group]
-        first, second = rows[2, group], rows[3, group]
+        if normal:
+            mean, inverse, second = rows[0, group], rows[1, group], rows[3, group]
+        if plain:
+            first = rows[2, group]
         for c in chunks:
             part = rebuilt[k, group, c * LANES : (c + 1) * LANES]
-            normed = (x[group, columns[c]].astype(F32) - mean) * inverse
             scaled = part * gains[c]
-            first = first + scaled
-            second = second + scaled * normed
-            products[c] = products[c] + fold(part * normed)
-            plain[c] = plain[c] + fold(part)
-        rows[2, group] = first
-        rows[3, group] = second
+            if plain:
+                first = first + scaled
+                bare[c] = bare[c] + fold(part)
+            if normal:
+                normed = (x[group, columns[c]].astype(F32) - mean) * inverse
+                second = second + scaled * normed
+                products[c] = products[c] + fold(part * normed)
+        if plain:
+            rows[2, group] = first
+        if normal:
+            rows[3, group] = second
     for c in chunks:
         lanes = slice(c * LANES, (c + 1) * LANES)
-        sums[k, 0:1, lanes] = jnp.sum(products[c], axis=0, keepdims=True)
-        sums[k, 1:2, lanes] = jnp.sum(plain[c], axis=0, keepdims=True)
+        if normal:
+            sums[k, 0:1, lanes] = jnp.sum(products[c], axis=0, keepdims=True)
+        if plain:
+            sums[k, 1:2, lanes] = jnp.sum(bare[c], axis=0, keepdims=True)
 
 
 def row_mean(total, features):
@@ -69,35 +79,46 @@
     left = left_out[...]
     rows[...] = jnp.zeros_like(rows)
 
-    @pl.loop(0, blocks)
-    def _(j):
+    for j in range(UNROLL):
         fetch(j).wait()
+    for r in range(0, tokens, GROUP):
+        group = slice(r, r + GROUP)
+        total = x[group, :LANES].astype(F32)
+        for c in chunks[1:]:
+            total = total + x[group, c * LANES : (c + 1) * LANES].astype(F32)
+        rows[0, group] = row_mean(total, width)
+
+    @pl.loop(0, blocks // UNROLL)
+    def _(step):
+        @pl.when(step > 0)
+        def _():
+            for u in range(UNROLL):
+                fetch(step * UNROLL + u).wait()
+
         for r in range(0, tokens, GROUP):
             group = slice(r, r + GROUP)
-            total = rows[0, group]
-            for c in chunks:
-                columns = pl.ds(pl.multiple_of(j * width + c * LANES, LANES), LANES)
-                total = total + x[group, columns].astype(F32)
-            rows[0, group] = total
-
-    rows[0] = row_mean(rows[0], features)
-
-    @pl.loop(0, blocks)
-    def _(j):
-        for r in range(0, tokens, GROUP):
-            group = slice(r, r + GROUP)
-            total, mean = rows[1, group], rows[0, group]
-            for c in chunks:
-                columns = pl.ds(pl.multiple_of(j * width + c * LANES, LANES), LANES)
-                center = x[group, columns].astype(F32) - mean
-                total = total + center * center
+            base, total, squares = rows[0, group], rows[1, group], rows[3, group]
+            for u in range(UNROLL):
+                for c in chunks:
+                    start = (step * UNROLL + u) * width + c * LANES
+                    center = x[group, pl.ds(pl.multiple_of(start, LANES), LANES)].astype(F32) - base
+                    total = total + center
+                    squares = squares + center * center
             rows[1, group] = total
-
-    rows[1] = lax.rsqrt(row_mean(rows[1], features) + 1e-05)
-
-    @pl.loop(0, half)
-    def _(k):
-        gain_pass(2 * k + parity[0], k, left, mine, x, gain, rows, rebuilt, sums)
+            rows[3, group] = squares
+        for k in [step * UNROLL // 2 + u for u in range(UNROLL // 2)]:
+            gain_pass(2 * k + parity[0], k, left, mine, x, gain, rows, rebuilt, sums, normal=False)
+
+    shift = row_mean(rows[1], features)
+    variance = jnp.maximum(row_mean(rows[3], features) - shift * shift, 0.0)
+    rows[0] = rows[0] + shift
+    rows[1] = lax.rsqrt(variance + 1e-05)
+    rows[3] = jnp.zeros((tokens, LANES), F32)
+
+    @pl.loop(0, half // UNROLL)
+    def _(step):
+        for k in [step * UNROLL + u for u in range(UNROLL)]:
+            gain_pass(2 * k + parity[0], k, left, mine, x, gain, rows, rebuilt, sums, plain=False)
 
 
 def second_kernel(
@@ -110,9 +131,10 @@
     left = left_ref[...]
     rows[...] = rows_in[...]
 
-    @pl.loop(0, half)
-    def _(k):
-        gain_pass(2 * k + (1 - parity[0]), k, left, theirs, x, gain, rows, rebuilt, sums)
+    @pl.loop(0, half // UNROLL)
+    def _(step):
+        for k in [step * UNROLL + u for u in range(UNROLL)]:
+            gain_pass(2 * k + (1 - parity[0]), k, left, theirs, x, gain, rows, rebuilt, sums)
 
     first = row_mean(rows[2], features)
     second = row_mean(rows[3], features)
@@ -124,20 +146,26 @@
             j = 2 * k + (parity[0] ^ side)
             columns = [pl.ds(pl.multiple_of(j * width + c * LANES, LANES), LANES) for c in chunks]
             gains = [jnp.broadcast_to(gain[:, columns[c]], (GROUP, LANES)) for c in chunks]
+            groups = []
             for r in range(0, tokens, GROUP):
                 group = slice(r, r + GROUP)
                 inverse, slope, offset = rows[1, group], rows[2, group], rows[3, group]
+                values = []
                 for c in chunks:
                     lanes = slice(c * LANES, (c + 1) * LANES)
                     scaled = source[k, group, lanes] * gains[c]
                     value = scaled * inverse - x[group, columns[c]].astype(F32) * slope + offset
-                    target[k, group, lanes] = value.astype(BF16)
-            return total + lax.dot_general(factors[k, rank:, :], target[k], NT, preferred_element_type=F32)
+                    values.append(value.astype(BF16))
+                    target[k, group, lanes] = values[-1]
+                groups.append(jnp.concatenate(values, axis=1))
+            block = jnp.concatenate(groups, axis=0)
+            return total + lax.dot_general(block, factors[k, rank:, :], NT, preferred_element_type=F32)
 
         return step
 
-    power = lax.fori_loop(0, half, project(0, mine, rebuilt_mine, kept), jnp.zeros((rank, tokens), F32))
-    power = lax.fori_loop(0, half, project(1, theirs, rebuilt, moved), power)
+    power = jnp.zeros((tokens, rank), F32)
+    power = lax.fori_loop(0, half, project(0, mine, rebuilt_mine, kept), power, unroll=UNROLL)
+    power = lax.fori_loop(0, half, project(1, theirs, rebuilt, moved), power, unroll=UNROLL).T
     power_t[...] = power
     gram = lax.dot_general(power, power, NT, precision=lax.Precision.HIGHEST, preferred_element_type=F32)
     side = rank // 2
@@ -157,12 +185,13 @@
     half, height, _ = out.shape
     rank = both.shape[0] // 2
 
-    @pl.loop(0, half)
-    def _(k):
-        terms = jnp.dot(both, boundary[k], preferred_element_type=F32)
-        out[k, :rank, :] = terms[:rank] + terms[rank:]
-        out[k, rank : rank + 2, :] = sums[k, 0:2, :]
-        out[k, rank + 2 :, :] = tail[: height - rank - 2]
+    @pl.loop(0, half // UNROLL)
+    def _(step):
+        for k in [step * UNROLL + u for u in range(UNROLL)]:
+            terms = jnp.dot(both, boundary[k], preferred_element_type=F32)
+            out[k, :rank, :] = terms[:rank] + terms[rank:]
+            out[k, rank : rank + 2, :] = sums[k, 0:2, :]
+            out[k, rank + 2 :, :] = tail[: height - rank - 2]
 
 
 def third_kernel(both, kept, sums, tail, keep):
@@ -229,6 +258,18 @@
     moved[:, width:] = jnp.dot(inverse, power_t[...], **exact).astype(BF16)
 
 
+def place_kernel(moved, left_out, right_out, sent):
+    width = right_out.shape[1]
+    copies = [
+        pltpu.make_async_copy(moved.at[:, :width], right_out, sent.at[0]),
+        pltpu.make_async_copy(moved.at[:, width:], left_out, sent.at[1]),
+    ]
+    for copy in copies:
+        copy.start()
+    for copy in copies:
+        copy.wait()
+
+
 def limit(mib):
     return pltpu.CompilerParams(vmem_limit_bytes=mib * 2**20)
 
@@ -248,6 +289,7 @@
     groups = [[2 * k + c for k in range(half)] for c in range(2)]
     shape = jax.ShapeDtypeStruct
 
+    x_hbm = pltpu.with_memory_space_constraint(saved_input[0], pltpu.HBM)
     own = jnp.concatenate([right_in[0].T, basis[0].T], axis=0)
     copies = jnp.broadcast_to(own[None], (half,) + own.shape)
     mine = lax.all_to_all(copies, "dp", 0, 0, tiled=True, axis_index_groups=groups)
@@ -267,7 +309,7 @@
         scratch_shapes=[pltpu.SemaphoreType.DMA((replicas,))],
         compiler_params=limit(20),
         cost_estimate=cost(24),
-    )(parity, saved_input[0], norm_gain, left_in[0].T, mine)
+    )(parity, x_hbm, norm_gain, left_in[0].T, mine)
     power_t, both, kept, tail, send = pl.pallas_call(
         second_kernel,
         out_shape=(
@@ -309,7 +351,15 @@
     )(terms, power_t)
     sections = lax.axis_size("section")
     moved = lax.ppermute(moved, "section", [(i, i - 1) for i in range(1, sections)])
-    return gain_grad, bias_grad, moved[:, width:].T[None], moved[:, :width].T[None]
+    left_out, right_out = pl.pallas_call(
+        place_kernel,
+        out_shape=(shape((rank, tokens), BF16), shape((rank, width), BF16)),
+        in_specs=[VMEM],
+        out_specs=(pl.BlockSpec(memory_space=pltpu.HBM),) * 2,
+        scratch_shapes=[pltpu.SemaphoreType.DMA((2,))],
+        compiler_params=limit(4),
+    )(moved)
+    return gain_grad, bias_grad, left_out.T[None], right_out.T[None]
 
 
 def solution(mesh):

time: 95.8 us -> 89.1 us (0.930)
  Pallas kernels: 18 us -> 13.7 us
  local copies, waits for them, and re-layouts: 3.25 us -> 0.12 us
    pallas_call x1, Pallas kernels: 8.46 us -> 4.83 us  [on_device(): pl.pallas_call(second_kernel, out_shape=(shape((rank, tokens), F32), shap...]
    unnamed x6 -> x4, local copies, waits for them, and re-layouts: 1.9 us -> 0.01 us
    broadcast_in_dim x2 -> x0, local copies, waits for them, and re-layouts: 1.25 us -> none  [the longest x1 0.65 us: on_device(): moved[:, :width].T[None]]
  transfers between devices with their start and end apart: 3 -> 3, of which waited for: 2 -> 2; matrix products, arithmetic and copies ran while one was open for 0% -> 0% of each run, Pallas kernels for 7% -> 6%
where the time goes in v3:
time: 89.1 us; the launch traced here: 87.6 us
  blocking collectives  54.1 us (61%)
  Pallas kernels  13.7 us (15%)
  waiting for transfers between devices  10.3 us (12%)
  starting transfers between devices  7.58 us (9%)
  other arithmetic  1.19 us (1%)
    all_to_all x1, blocking collectives, on_device(): lax.all_to_all(copies, 'dp', 0, 0, tiled=True, axis_index_groups=groups)  27.5 us
    all_to_all x1, blocking collectives, on_device(): lax.all_to_all(keep + other, 'dp', 0, 0, tiled=True, axis_index_groups=gr...  26.6 us
    ppermute x1, waiting for transfers between devices, on_device(): lax.ppermute(moved, 'section', [(i, i - 1) for i in range(1, sections)])  7.71 us
    pallas_call x1, Pallas kernels, on_device(): pl.pallas_call(second_kernel, out_shape=(shape((rank, tokens), F32), shap...  4.83 us
    pallas_call x1, Pallas kernels, on_device(): pl.pallas_call(first_kernel, out_shape=(shape((tokens, features), BF16),...  4.51 us
    ppermute x1, starting transfers between devices, on_device(): lax.ppermute(moved, 'section', [(i, i - 1) for i in range(1, sections)])  3.24 us
    pallas_call x1, Pallas kernels, on_device(): pl.pallas_call(lambda *refs: post_kernel(factor, *refs), out_shape=(shape...  2.92 us
    ppermute x1, waiting for transfers between devices, on_device(): other = lax.ppermute(send, 'dp', others)  2.56 us
  transfers between devices with their start and end apart: 3, of which 2 were waited for; matrix products, arithmetic and copies ran while one was open for 0% of the time, Pallas kernels for 6%

profile of v3, /device:TPU:56, one launch (start us, length us, event | category | flops | bytes accessed | tf_op | source)
XLA Modules:
  0.0 87.6 jit_solution(16522085549659042582)
XLA Ops:
  0.6 1.0 %pad_maximum_fusion = bf16[128,768]{1,0:T(8,128)(2,1)S(1)} fusion(bf16[64,768]{1,0:T(8,128)(2,1)} %bitcast.19, bf16[64,768]{1,0:T(8,128)(2,1)} %bitcast.20), kind=kLoop, calls=%fused_computation | loop fusion | flops 393216 | bytes 393216 | tf_op jit(solution)/shard_map/concatenate | solution.py:293
  1.6 0.1 broadcast_in_dim.12
  1.7 0.0 copy-start
  1.7 0.0 copy-start.1
  1.7 27.5 %all_to_all.10.mine = bf16[8,128,768]{2,1,0:T(8,128)(2,1)S(1)} all-to-all(bf16[8,128,768]{2,1,0:T(8,128)(2,1)S(1)} %broadcast_in_dim.12), channel_id=1, replica_groups={{0,2,4,6,8,10,12,14},{1,3,5,7,9,11,13,15},{16,18,20,22,24,26,28,30},{17..., dimensions={0} | all-to-all | bytes 3145728 | tf_op jit(solution)/shard_map/all_to_all | solution.py:295
  29.2 1.9 %collective-permute-start = (bf16[8,128,768]{2,1,0:T(8,128)(2,1)S(1)}, bf16[8,128,768]{2,1,0:T(8,128)(2,1)S(1)}, u32[]{:S(2)}, u32[]{:S(2)}) collective-permute-start(bf16[8,128,768]{2,1,0:T(8,128)(2,1)S(1)} %all_to_all.10.mine), channel_id=1, source_target_pairs={{0,1},{1,0},{2,3},{3,2},{4,5},{5,4},{6,7},{7,6},{8,9},{9,8},{10,11... | collective-permute-start | bytes 4718600 | tf_op jit(solution)/shard_map/ppermute | solution.py:296
  31.2 0.0 copy-done
  31.2 0.0 copy-done.1
  31.2 4.5 %shard_map.84 = (bf16[128,12288]{1,0:T(8,128)(2,1)S(1)}, bf16[128,64]{1,0:T(8,128)(2,1)S(1)}, f32[4,128,128]{2,1,0:T(8,128)S(1)}, f32[8,128,768]{2,1,0:T(8,128)S(1)}, f32[8,8,768]{2,1,0:T(8,128)S(1)}) custom-call(s32[1]{0:T(128)} %bitcast.parity, bf16[128,12288]{1,0:T(8,128)(2,1)} %bitcast.18, f32[1,12288]{1,0:T(1,128)S(1)} %copy-done, ...), custom_call_target="tpu_custom_call" | custom-call | bytes 25165824 | tf_op jit(solution)/shard_map/pallas_call | solution.py:298
  35.7 0.0 collective-permute-done.theirs
  35.7 4.8 %shard_map.85 = (f32[64,128]{1,0:T(8,128)S(1)}, bf16[128,128]{1,0:T(8,128)(2,1)S(1)}, bf16[8,128,768]{2,1,0:T(8,128)(2,1)S(1)}, f32[8,768]{1,0:T(8,128)S(1)}, f32[8,72,768]{2,1,0:T(8,128)S(1)}) custom-call(s32[1]{0:T(128)} %bitcast.parity, bf16[128,12288]{1,0:T(8,128)(2,1)S(1)} %get-tuple-element.19.x, f32[1,12288]{1,0:T(1,128)S(1)} %copy-done, ...), custom_call_target="tpu_custom_call" | custom-call | tf_op jit(solution)/shard_map/pallas_call | solution.py:313
  40.6 2.4 %collective-permute-start.1 = (f32[8,72,768]{2,1,0:T(8,128)S(1)}, f32[8,72,768]{2,1,0:T(8,128)S(1)}, u32[]{:S(2)}, u32[]{:S(2)}) collective-permute-start(f32[8,72,768]{2,1,0:T(8,128)S(1)} %get-tuple-element.27), channel_id=1, source_target_pairs={{0,1},{1,0},{2,3},{3,2},{4,5},{5,4},{6,7},{7,6},{8,9},{9,8},{10,11... | collective-permute-start | bytes 5308424 | tf_op jit(solution)/shard_map/ppermute | solution.py:332
  43.0 0.7 shard_map.86
  43.7 2.6 %collective-permute-done.1 = f32[8,72,768]{2,1,0:T(8,128)S(1)} collective-permute-done((f32[8,72,768]{2,1,0:T(8,128)S(1)}, f32[8,72,768]{2,1,0:T(8,128)S(1)}, u32[]{:S(2)}, u32[]{:S(2)}) %collective-permute-start.1) | collective-permute-done | bytes 1769504 | tf_op jit(solution)/shard_map/ppermute | solution.py:332
  46.3 0.2 add.3
  46.5 26.6 %all_to_all.11.refs_0_ = f32[8,72,768]{2,1,0:T(8,128)S(1)} all-to-all(f32[8,72,768]{2,1,0:T(8,128)S(1)} %add.3), channel_id=1, replica_groups={{0,2,4,6,8,10,12,14},{1,3,5,7,9,11,13,15},{16,18,20,22,24,26,28,30},{17..., dimensions={0} | all-to-all | bytes 3538944 | tf_op jit(solution)/shard_map/all_to_all | solution.py:341
  73.1 2.9 %shard_map.87 = (f32[1,768]{1,0:T(1,128)}, f32[1,768]{1,0:T(1,128)}, bf16[64,896]{1,0:T(8,128)(2,1)S(1)}) custom-call(f32[8,72,768]{2,1,0:T(8,128)S(1)} %all_to_all.11.refs_0_, f32[64,128]{1,0:T(8,128)S(1)} %get-tuple-element.28.refs_1_), custom_call_target="tpu_custom_call" | custom-call | tf_op jit(solution)/shard_map/pallas_call | solution.py:344
  76.0 3.2 %collective-permute-start.2 = (bf16[64,896]{1,0:T(8,128)(2,1)S(1)}, bf16[64,896]{1,0:T(8,128)(2,1)S(1)}, u32[]{:S(2)}, u32[]{:S(2)}) collective-permute-start(bf16[64,896]{1,0:T(8,128)(2,1)S(1)} %get-tuple-element.31), channel_id=1, source_target_pairs={{16,0},{32,16},{48,32},{64,48},{80,64},{96,80},{112,96},{128,112},... | collective-permute-start | bytes 344072 | tf_op jit(solution)/shard_map/ppermute | solution.py:353
  79.3 7.7 %collective-permute-done.2.moved = bf16[64,896]{1,0:T(8,128)(2,1)S(1)} collective-permute-done((bf16[64,896]{1,0:T(8,128)(2,1)S(1)}, bf16[64,896]{1,0:T(8,128)(2,1)S(1)}, u32[]{:S(2)}, u32[]{:S(2)}) %collective-permute-start.2) | collective-permute-done | bytes 114720 | tf_op jit(solution)/shard_map/ppermute | solution.py:353
  87.0 0.7 shard_map.88
Async XLA Ops:
  1.7 29.5 %copy-start = (f32[1,12288]{1,0:T(1,128)S(1)}, f32[1,12288]{1,0:T(1,128)}, u32[]{:S(2)}) copy-start(f32[1,12288]{1,0:T(1,128)} %gain.3) | copy-start | bytes 147460
  1.7 29.5 %copy-start.1 = (bf16[1,128,64]{1,2,0:T(8,128)(2,1)S(1)}, bf16[1,128,64]{1,2,0:T(8,128)(2,1)}, u32[]{:S(2)}) copy-start(bf16[1,128,64]{1,2,0:T(8,128)(2,1)} %param.7) | copy-start | bytes 49156
  29.2 6.5 %collective-permute-start = (bf16[8,128,768]{2,1,0:T(8,128)(2,1)S(1)}, bf16[8,128,768]{2,1,0:T(8,128)(2,1)S(1)}, u32[]{:S(2)}, u32[]{:S(2)}) collective-permute-start(bf16[8,128,768]{2,1,0:T(8,128)(2,1)S(1)} %all_to_all.10.mine), channel_id=1, source_target_pairs={{0,1},{1,0},{2,3},{3,2},{4,5},{5,4},{6,7},{7,6},{8,9},{9,8},{10,11... | collective-permute-start | bytes 4718600 | tf_op jit(solution)/shard_map/ppermute | solution.py:296
  40.6 5.7 %collective-permute-start.1 = (f32[8,72,768]{2,1,0:T(8,128)S(1)}, f32[8,72,768]{2,1,0:T(8,128)S(1)}, u32[]{:S(2)}, u32[]{:S(2)}) collective-permute-start(f32[8,72,768]{2,1,0:T(8,128)S(1)} %get-tuple-element.27), channel_id=1, source_target_pairs={{0,1},{1,0},{2,3},{3,2},{4,5},{5,4},{6,7},{7,6},{8,9},{9,8},{10,11... | collective-permute-start | bytes 5308424 | tf_op jit(solution)/shard_map/ppermute | solution.py:332
  76.0 11.0 %collective-permute-start.2 = (bf16[64,896]{1,0:T(8,128)(2,1)S(1)}, bf16[64,896]{1,0:T(8,128)(2,1)S(1)}, u32[]{:S(2)}, u32[]{:S(2)}) collective-permute-start(bf16[64,896]{1,0:T(8,128)(2,1)S(1)} %get-tuple-element.31), channel_id=1, source_target_pairs={{16,0},{32,16},{48,32},{64,48},{80,64},{96,80},{112,96},{128,112},... | collective-permute-start | bytes 344072 | tf_op jit(solution)/shard_map/ppermute | solution.py:353

commit v4 on v3

--- a/solution.py
+++ b/solution.py
@@ -11,6 +11,7 @@
 F32 = jnp.float32
 BF16 = jnp.bfloat16
 NT = (((1,), (1,)), ((), ()))
+EXACT = dict(precision=lax.Precision.HIGHEST, preferred_element_type=F32)
 VMEM = pl.BlockSpec(memory_space=pltpu.VMEM)
 SMEM = pl.BlockSpec(memory_space=pltpu.SMEM)
 
@@ -122,7 +123,7 @@
 
 
 def second_kernel(
-    parity, x, gain, left_ref, rows_in, rebuilt_mine, mine, theirs, power_t, both_out, kept, tail, send, rows, rebuilt, sums, moved
+    parity, x, gain, left_ref, rows_in, rebuilt_mine, mine, theirs, power_t, kept, packed, send, rows, rebuilt, sums, moved, tail
 ):
     half, height, width = theirs.shape
     tokens, features = x.shape
@@ -130,6 +131,21 @@
     chunks = range(width // LANES)
     left = left_ref[...]
     rows[...] = rows_in[...]
+
+    def mixing(k, total):
+        terms = []
+        for side, factors in enumerate((mine, theirs)):
+            start = (2 * k + (parity[0] ^ side)) * width
+            scaled = factors[k, :rank, :].astype(F32) * gain[:, pl.ds(pl.multiple_of(start, LANES), width)]
+            terms.append(lax.dot_general(factors[k, rank:, :], scaled.astype(BF16), NT, preferred_element_type=F32))
+        return total + (terms[0] + terms[1])
+
+    mixed = lax.fori_loop(0, half, mixing, jnp.zeros((rank, rank), F32), unroll=UNROLL)
+    near = lax.dot_general(mixed, mixed, NT, **EXACT)
+    row = lax.broadcasted_iota(jnp.int32, near.shape, 0)
+    col = lax.broadcasted_iota(jnp.int32, near.shape, 1)
+    level = jnp.sum(mixed * mixed) * (1e-06 / rank) + 1e-08
+    basis_change = inverse_factor(near + jnp.where(row == col, level, 0.0))
 
     @pl.loop(0, half // UNROLL)
     def _(step):
@@ -165,37 +181,86 @@
 
     power = jnp.zeros((tokens, rank), F32)
     power = lax.fori_loop(0, half, project(0, mine, rebuilt_mine, kept), power, unroll=UNROLL)
-    power = lax.fori_loop(0, half, project(1, theirs, rebuilt, moved), power, unroll=UNROLL).T
+    power = lax.fori_loop(0, half, project(1, theirs, rebuilt, moved), power, unroll=UNROLL)
+    power = lax.dot_general(basis_change, power, NT, **EXACT)
     power_t[...] = power
-    gram = lax.dot_general(power, power, NT, precision=lax.Precision.HIGHEST, preferred_element_type=F32)
-    side = rank // 2
-    tail[...] = jnp.zeros_like(tail)
-    packed = jnp.concatenate([gram[:side], gram[side:]], axis=1)
-    per = width // LANES
-    for q in range(side):
-        tail[q // per : q // per + 1, (q % per) * LANES : (q % per + 1) * LANES] = packed[q : q + 1]
+    pack(lax.dot_general(power, power, NT, **EXACT), packed)
     high = power.astype(BF16)
-    low = (power - high.astype(F32)).astype(BF16)
-    both = jnp.concatenate([high, low], axis=0)
-    both_out[...] = both
-    feature_terms(both, moved, sums, tail, send)
-
-
-def feature_terms(both, boundary, sums, tail, out):
-    half, height, _ = out.shape
-    rank = both.shape[0] // 2
+    split_gram(packed[0:4, :], tail)
 
     @pl.loop(0, half // UNROLL)
     def _(step):
         for k in [step * UNROLL + u for u in range(UNROLL)]:
-            terms = jnp.dot(both, boundary[k], preferred_element_type=F32)
-            out[k, :rank, :] = terms[:rank] + terms[rank:]
-            out[k, rank : rank + 2, :] = sums[k, 0:2, :]
-            out[k, rank + 2 :, :] = tail[: height - rank - 2]
-
-
-def third_kernel(both, kept, sums, tail, keep):
-    feature_terms(both[...], kept, sums, tail, keep)
+            terms = jnp.dot(high, moved[k], preferred_element_type=F32)
+            send[k, :rank, :] = terms.astype(BF16)
+            split_sums(sums[k, 0:2, :], tail)
+            send[k, rank:, :] = tail[...].astype(BF16)
+
+
+def split(value, count):
+    terms = []
+    for _ in range(count):
+        terms.append(value.astype(BF16).astype(F32))
+        value = value - terms[-1]
+    return terms
+
+
+def split_sums(value, tail):
+    for i, term in enumerate(split(value, 2)):
+        tail[2 * i : 2 * i + 2, :] = term
+
+
+def split_gram(value, tail):
+    for i, term in enumerate(split(value, 3)):
+        tail[4 + 4 * i : 8 + 4 * i, :] = term
+
+
+def pack(gram, packed):
+    size = gram.shape[0]
+    half, quarter = size // 2, size // 4
+    per = packed.shape[1] // LANES
+    corner = gram[half:, half:]
+    upper = jnp.concatenate([gram[:quarter], gram[quarter:half]], axis=1)
+    lower = jnp.concatenate([corner[8 * i : 8 * i + 8] for i in range(half // 8)], axis=1)
+    packed[...] = jnp.zeros_like(packed)
+    for q in range(quarter + 8):
+        line = upper[q : q + 1] if q < quarter else lower[q - quarter : q - quarter + 1]
+        packed[q // per : q // per + 1, (q % per) * LANES : (q % per + 1) * LANES] = line
+
+
+def unpack(packed, square):
+    lines = square.shape[0]
+    per = packed.shape[1] // LANES
+    quarter = lines - 8
+    half = 2 * quarter
+    for q in range(lines):
+        square[q : q + 1, :] = packed[q // per : q // per + 1, (q % per) * LANES : (q % per + 1) * LANES]
+    upper = jnp.concatenate([square[:quarter, : 2 * half], square[:quarter, 2 * half :]], axis=0)
+    corner = jnp.concatenate([square[quarter:, half * i : half * (i + 1)] for i in range(half // 8)], axis=0)
+    return jnp.concatenate([upper, jnp.concatenate([upper[:, half:].T, corner], axis=1)], axis=0)
+
+
+def third_kernel(power_t, kept, keep):
+    high = power_t[...].astype(BF16)
+
+    @pl.loop(0, keep.shape[0] // UNROLL)
+    def _(step):
+        for k in [step * UNROLL + u for u in range(UNROLL)]:
+            keep[k] = jnp.dot(high, kept[k], preferred_element_type=F32)
+
+
+def pair_kernel(keep, packed, sums, other, out, tail):
+    half, rank, _ = keep.shape
+    theirs = other[0, rank:, :].astype(F32)
+    split_gram(packed[0:4, :] + (theirs[4:8] + (theirs[8:12] + theirs[12:16])), tail)
+
+    @pl.loop(0, half // UNROLL)
+    def _(step):
+        for k in [step * UNROLL + u for u in range(UNROLL)]:
+            out[k, :rank, :] = (keep[k] + other[k, :rank, :].astype(F32)).astype(BF16)
+            theirs = other[k, rank:, :].astype(F32)
+            split_sums(sums[k, 0:2, :] + (theirs[0:2] + theirs[2:4]), tail)
+            out[k, rank:, :] = tail[...].astype(BF16)
 
 
 def inverse_factor(gram):
@@ -240,22 +305,15 @@
 def post_kernel(factor, terms, power_t, gain_out, bias_out, moved, square):
     rank, tokens = power_t.shape
     width = terms.shape[2]
-    chunks = width // LANES
-    half = rank // 2
-    total = terms[0]
+    total = terms[0].astype(F32)
     for j in range(1, terms.shape[0]):
-        total = total + terms[j]
-    gain_out[...] = total[rank : rank + 1] * factor
-    bias_out[...] = total[rank + 1 : rank + 2] * factor
-    for q in range(half):
-        line = rank + 2 + q // chunks
-        start = (q % chunks) * LANES
-        square[q : q + 1, :] = total[line : line + 1, start : start + LANES]
-    packed = square[...]
-    inverse = inverse_factor(jnp.concatenate([packed[:, :rank], packed[:, rank:]], axis=0))
-    exact = dict(precision=lax.Precision.HIGHEST, preferred_element_type=F32)
-    moved[:, :width] = jnp.dot(inverse, total[:rank], **exact).astype(BF16)
-    moved[:, width:] = jnp.dot(inverse, power_t[...], **exact).astype(BF16)
+        total = total + terms[j].astype(F32)
+    extra = total[rank:]
+    gain_out[...] = (extra[0:1] + extra[2:3]) * factor
+    bias_out[...] = (extra[1:2] + extra[3:4]) * factor
+    inverse = inverse_factor(unpack(extra[4:8] + (extra[8:12] + extra[12:16]), square))
+    moved[:, :width] = jnp.dot(inverse, total[:rank], **EXACT).astype(BF16)
+    moved[:, width:] = jnp.dot(inverse, power_t[...], **EXACT).astype(BF16)
 
 
 def place_kernel(moved, left_out, right_out, sent):
@@ -283,8 +341,7 @@
     width, rank = right_in.shape[1:]
     replicas = lax.axis_size("dp")
     half = replicas // 2
-    chunks = width // LANES
-    height = rank + 2 + -(-(rank // 2) // chunks)
+    height = rank + 16
     others = [(i, i ^ 1) for i in range(replicas)]
     groups = [[2 * k + c for k in range(half)] for c in range(2)]
     shape = jax.ShapeDtypeStruct
@@ -310,35 +367,43 @@
         compiler_params=limit(20),
         cost_estimate=cost(24),
     )(parity, x_hbm, norm_gain, left_in[0].T, mine)
-    power_t, both, kept, tail, send = pl.pallas_call(
+    power_t, kept, packed, send = pl.pallas_call(
         second_kernel,
         out_shape=(
             shape((rank, tokens), F32),
-            shape((2 * rank, tokens), BF16),
             shape((half, tokens, width), BF16),
             shape((8, width), F32),
-            shape((half, height, width), F32),
+            shape((half, height, width), BF16),
         ),
         in_specs=[SMEM] + [VMEM] * 7,
-        out_specs=(VMEM,) * 5,
+        out_specs=(VMEM,) * 4,
         scratch_shapes=[
             pltpu.VMEM((4, tokens, LANES), F32),
             pltpu.VMEM((half, tokens, width), F32),
             pltpu.VMEM((half, 8, width), F32),
             pltpu.VMEM((half, tokens, width), BF16),
+            pltpu.VMEM((16, width), F32),
         ],
         compiler_params=limit(32),
     )(parity, x, norm_gain, left, rows, rebuilt, mine, theirs)
     other = lax.ppermute(send, "dp", others)
     keep = pl.pallas_call(
         third_kernel,
-        out_shape=shape((half, height, width), F32),
-        in_specs=[VMEM] * 4,
+        out_shape=shape((half, rank, width), F32),
+        in_specs=[VMEM] * 2,
         out_specs=VMEM,
         compiler_params=limit(12),
         cost_estimate=cost(12),
-    )(both, kept, sums, tail)
-    terms = lax.all_to_all(keep + other, "dp", 0, 0, tiled=True, axis_index_groups=groups)
+    )(power_t, kept)
+    payload = pl.pallas_call(
+        pair_kernel,
+        out_shape=shape((half, height, width), BF16),
+        in_specs=[VMEM] * 4,
+        out_specs=VMEM,
+        scratch_shapes=[pltpu.VMEM((16, width), F32)],
+        compiler_params=limit(12),
+    )(keep, packed, sums, other)
+    terms = lax.all_to_all(payload, "dp", 0, 0, tiled=True, axis_index_groups=groups)
 
     factor = float(1.0 / (tokens * replicas) ** 0.5)
     gain_grad, bias_grad, moved = pl.pallas_call(
@@ -346,7 +411,7 @@
         out_shape=(shape((1, width), F32), shape((1, width), F32), shape((rank, width + tokens), BF16)),
         in_specs=[VMEM, VMEM],
         out_specs=(VMEM,) * 3,
-        scratch_shapes=[pltpu.VMEM((rank // 2, LANES), F32)],
+        scratch_shapes=[pltpu.VMEM((24, LANES), F32)],
         compiler_params=limit(16),
     )(terms, power_t)
     sections = lax.axis_size("section")

time: 89.1 us -> 82.8 us (0.929)
  blocking collectives: 54.1 us -> 45.6 us
  Pallas kernels: 13.7 us -> 16.9 us
  waiting for transfers between devices: 10.3 us -> 9.38 us
    all_to_all x1, blocking collectives: 26.6 us -> 18.1 us  [on_device(): lax.all_to_all(payload, 'dp', 0, 0, tiled=True, axis_index_groups=groups)]
    pallas_call x1, Pallas kernels: 4.83 us -> 7.87 us  [on_device(): pl.pallas_call(second_kernel, out_shape=(shape((rank, tokens), F32), shap...]
    ppermute x1, waiting for transfers between devices: 2.56 us -> 1.65 us  [on_device(): other = lax.ppermute(send, 'dp', others)]
where the time goes in v4:
time: 82.8 us; the launch traced here: 81.3 us
  blocking collectives  45.6 us (55%)
  Pallas kernels  16.9 us (20%)
  waiting for transfers between devices  9.38 us (11%)
  starting transfers between devices  7.58 us (9%)
  other arithmetic  0.96 us (1%)
    all_to_all x1, blocking collectives, on_device(): lax.all_to_all(copies, 'dp', 0, 0, tiled=True, axis_index_groups=groups)  27.5 us
    all_to_all x1, blocking collectives, on_device(): lax.all_to_all(payload, 'dp', 0, 0, tiled=True, axis_index_groups=groups)  18.1 us
    pallas_call x1, Pallas kernels, on_device(): pl.pallas_call(second_kernel, out_shape=(shape((rank, tokens), F32), shap...  7.87 us
    ppermute x1, waiting for transfers between devices, on_device(): lax.ppermute(moved, 'section', [(i, i - 1) for i in range(1, sections)])  7.73 us
    pallas_call x1, Pallas kernels, on_device(): pl.pallas_call(first_kernel, out_shape=(shape((tokens, features), BF16),...  4.51 us
    ppermute x1, starting transfers between devices, on_device(): lax.ppermute(moved, 'section', [(i, i - 1) for i in range(1, sections)])  3.23 us
    pallas_call x1, Pallas kernels, on_device(): pl.pallas_call(lambda *refs: post_kernel(factor, *refs), out_shape=(shape...  3.06 us
    ppermute x1, starting transfers between devices, on_device(): other = lax.ppermute(send, 'dp', others)  2.44 us
  transfers between devices with their start and end apart: 3, of which 2 were waited for; matrix products, arithmetic and copies ran while one was open for 0% of the time, Pallas kernels for 6%

profile of v4, /device:TPU:56, one launch (start us, length us, event | category | flops | bytes accessed | tf_op | source)
XLA Modules:
  0.0 81.3 jit_solution(16036894037786112556)
XLA Ops:
  0.6 1.0 %pad_maximum_fusion = bf16[128,768]{1,0:T(8,128)(2,1)S(1)} fusion(bf16[64,768]{1,0:T(8,128)(2,1)} %bitcast.19, bf16[64,768]{1,0:T(8,128)(2,1)} %bitcast.20), kind=kLoop, calls=%fused_computation | loop fusion | flops 393216 | bytes 393216 | tf_op jit(solution)/shard_map/concatenate | solution.py:350
  1.6 0.1 broadcast_in_dim.12
  1.7 0.0 copy-start
  1.7 0.0 copy-start.1
  1.7 27.5 %all_to_all.10.mine = bf16[8,128,768]{2,1,0:T(8,128)(2,1)S(1)} all-to-all(bf16[8,128,768]{2,1,0:T(8,128)(2,1)S(1)} %broadcast_in_dim.12), channel_id=1, replica_groups={{0,2,4,6,8,10,12,14},{1,3,5,7,9,11,13,15},{16,18,20,22,24,26,28,30},{17..., dimensions={0} | all-to-all | bytes 3145728 | tf_op jit(solution)/shard_map/all_to_all | solution.py:352
  29.2 1.9 %collective-permute-start = (bf16[8,128,768]{2,1,0:T(8,128)(2,1)S(1)}, bf16[8,128,768]{2,1,0:T(8,128)(2,1)S(1)}, u32[]{:S(2)}, u32[]{:S(2)}) collective-permute-start(bf16[8,128,768]{2,1,0:T(8,128)(2,1)S(1)} %all_to_all.10.mine), channel_id=1, source_target_pairs={{0,1},{1,0},{2,3},{3,2},{4,5},{5,4},{6,7},{7,6},{8,9},{9,8},{10,11... | collective-permute-start | bytes 4718600 | tf_op jit(solution)/shard_map/ppermute | solution.py:353
  31.2 0.0 copy-done
  31.2 0.0 copy-done.1
  31.2 4.5 %shard_map.84 = (bf16[128,12288]{1,0:T(8,128)(2,1)S(1)}, bf16[128,64]{1,0:T(8,128)(2,1)S(1)}, f32[4,128,128]{2,1,0:T(8,128)S(1)}, f32[8,128,768]{2,1,0:T(8,128)S(1)}, f32[8,8,768]{2,1,0:T(8,128)S(1)}) custom-call(s32[1]{0:T(128)} %bitcast.parity, bf16[128,12288]{1,0:T(8,128)(2,1)} %bitcast.18, f32[1,12288]{1,0:T(1,128)S(1)} %copy-done, ...), custom_call_target="tpu_custom_call" | custom-call | bytes 25165824 | tf_op jit(solution)/shard_map/pallas_call | solution.py:355
  35.7 0.0 collective-permute-done.theirs
  35.7 7.9 %shard_map.85 = (f32[64,128]{1,0:T(8,128)S(1)}, bf16[8,128,768]{2,1,0:T(8,128)(2,1)S(1)}, f32[8,768]{1,0:T(8,128)S(1)}, bf16[8,80,768]{2,1,0:T(8,128)(2,1)S(1)}) custom-call(s32[1]{0:T(128)} %bitcast.parity, bf16[128,12288]{1,0:T(8,128)(2,1)S(1)} %get-tuple-element.18.x, f32[1,12288]{1,0:T(1,128)S(1)} %copy-done, ...), custom_call_target="tpu_custom_call" | custom-call | tf_op jit(solution)/shard_map/pallas_call | solution.py:370
  43.6 2.4 %collective-permute-start.1 = (bf16[8,80,768]{2,1,0:T(8,128)(2,1)S(1)}, bf16[8,80,768]{2,1,0:T(8,128)(2,1)S(1)}, u32[]{:S(2)}, u32[]{:S(2)}) collective-permute-start(bf16[8,80,768]{2,1,0:T(8,128)(2,1)S(1)} %get-tuple-element.26), channel_id=1, source_target_pairs={{0,1},{1,0},{2,3},{3,2},{4,5},{5,4},{6,7},{7,6},{8,9},{9,8},{10,11... | collective-permute-start | bytes 2949128 | tf_op jit(solution)/shard_map/ppermute | solution.py:389
  46.0 0.5 shard_map.86.keep
  46.6 1.6 %collective-permute-done.1.other = bf16[8,80,768]{2,1,0:T(8,128)(2,1)S(1)} collective-permute-done((bf16[8,80,768]{2,1,0:T(8,128)(2,1)S(1)}, bf16[8,80,768]{2,1,0:T(8,128)(2,1)S(1)}, u32[]{:S(2)}, u32[]{:S(2)}) %collective-permute-start.1) | collective-permute-done | bytes 983072 | tf_op jit(solution)/shard_map/ppermute | solution.py:389
  48.2 0.3 shard_map.87
  48.5 18.1 %all_to_all.11.refs_0_ = bf16[8,80,768]{2,1,0:T(8,128)(2,1)S(1)} all-to-all(bf16[8,80,768]{2,1,0:T(8,128)(2,1)S(1)} %shard_map.87), channel_id=1, replica_groups={{0,2,4,6,8,10,12,14},{1,3,5,7,9,11,13,15},{16,18,20,22,24,26,28,30},{17..., dimensions={0} | all-to-all | bytes 1966080 | tf_op jit(solution)/shard_map/all_to_all | solution.py:406
  66.6 3.1 %shard_map.88 = (f32[1,768]{1,0:T(1,128)}, f32[1,768]{1,0:T(1,128)}, bf16[64,896]{1,0:T(8,128)(2,1)S(1)}) custom-call(bf16[8,80,768]{2,1,0:T(8,128)(2,1)S(1)} %all_to_all.11.refs_0_, f32[64,128]{1,0:T(8,128)S(1)} %get-tuple-element.22.power_t.refs_1_), custom_call_target="tpu_custom_call" | custom-call | tf_op jit(solution)/shard_map/pallas_call | solution.py:409
  69.7 3.2 %collective-permute-start.2 = (bf16[64,896]{1,0:T(8,128)(2,1)S(1)}, bf16[64,896]{1,0:T(8,128)(2,1)S(1)}, u32[]{:S(2)}, u32[]{:S(2)}) collective-permute-start(bf16[64,896]{1,0:T(8,128)(2,1)S(1)} %get-tuple-element.29), channel_id=1, source_target_pairs={{16,0},{32,16},{48,32},{64,48},{80,64},{96,80},{112,96},{128,112},... | collective-permute-start | bytes 344072 | tf_op jit(solution)/shard_map/ppermute | solution.py:418
  72.9 7.7 %collective-permute-done.2.moved = bf16[64,896]{1,0:T(8,128)(2,1)S(1)} collective-permute-done((bf16[64,896]{1,0:T(8,128)(2,1)S(1)}, bf16[64,896]{1,0:T(8,128)(2,1)S(1)}, u32[]{:S(2)}, u32[]{:S(2)}) %collective-permute-start.2) | collective-permute-done | bytes 114720 | tf_op jit(solution)/shard_map/ppermute | solution.py:418
  80.7 0.7 shard_map.89
Async XLA Ops:
  1.7 29.5 %copy-start = (f32[1,12288]{1,0:T(1,128)S(1)}, f32[1,12288]{1,0:T(1,128)}, u32[]{:S(2)}) copy-start(f32[1,12288]{1,0:T(1,128)} %gain.3) | copy-start | bytes 147460
  1.7 29.5 %copy-start.1 = (bf16[1,128,64]{1,2,0:T(8,128)(2,1)S(1)}, bf16[1,128,64]{1,2,0:T(8,128)(2,1)}, u32[]{:S(2)}) copy-start(bf16[1,128,64]{1,2,0:T(8,128)(2,1)} %param.7) | copy-start | bytes 49156
  29.2 6.5 %collective-permute-start = (bf16[8,128,768]{2,1,0:T(8,128)(2,1)S(1)}, bf16[8,128,768]{2,1,0:T(8,128)(2,1)S(1)}, u32[]{:S(2)}, u32[]{:S(2)}) collective-permute-start(bf16[8,128,768]{2,1,0:T(8,128)(2,1)S(1)} %all_to_all.10.mine), channel_id=1, source_target_pairs={{0,1},{1,0},{2,3},{3,2},{4,5},{5,4},{6,7},{7,6},{8,9},{9,8},{10,11... | collective-permute-start | bytes 4718600 | tf_op jit(solution)/shard_map/ppermute | solution.py:353
  43.6 4.6 %collective-permute-start.1 = (bf16[8,80,768]{2,1,0:T(8,128)(2,1)S(1)}, bf16[8,80,768]{2,1,0:T(8,128)(2,1)S(1)}, u32[]{:S(2)}, u32[]{:S(2)}) collective-permute-start(bf16[8,80,768]{2,1,0:T(8,128)(2,1)S(1)} %get-tuple-element.26), channel_id=1, source_target_pairs={{0,1},{1,0},{2,3},{3,2},{4,5},{5,4},{6,7},{7,6},{8,9},{9,8},{10,11... | collective-permute-start | bytes 2949128 | tf_op jit(solution)/shard_map/ppermute | solution.py:389
  69.7 11.0 %collective-permute-start.2 = (bf16[64,896]{1,0:T(8,128)(2,1)S(1)}, bf16[64,896]{1,0:T(8,128)(2,1)S(1)}, u32[]{:S(2)}, u32[]{:S(2)}) collective-permute-start(bf16[64,896]{1,0:T(8,128)(2,1)S(1)} %get-tuple-element.29), channel_id=1, source_target_pairs={{16,0},{32,16},{48,32},{64,48},{80,64},{96,80},{112,96},{128,112},... | collective-permute-start | bytes 344072 | tf_op jit(solution)/shard_map/ppermute | solution.py:418

commit v5 on v4

--- a/solution.py
+++ b/solution.py
@@ -7,7 +7,8 @@
 
 LANES = 128
 GROUP = 16
-UNROLL = 4
+UNROLL = 8
+FETCH = 2
 F32 = jnp.float32
 BF16 = jnp.bfloat16
 NT = (((1,), (1,)), ((), ()))
@@ -80,7 +81,12 @@
     left = left_out[...]
     rows[...] = jnp.zeros_like(rows)
 
-    for j in range(UNROLL):
+    @pl.loop(0, half // UNROLL)
+    def _(step):
+        for k in [step * UNROLL + u for u in range(UNROLL)]:
+            gain_pass(2 * k + parity[0], k, left, mine, x, gain, rows, rebuilt, sums, normal=False)
+
+    for j in range(FETCH):
         fetch(j).wait()
     for r in range(0, tokens, GROUP):
         group = slice(r, r + GROUP)
@@ -89,26 +95,24 @@
             total = total + x[group, c * LANES : (c + 1) * LANES].astype(F32)
         rows[0, group] = row_mean(total, width)
 
-    @pl.loop(0, blocks // UNROLL)
+    @pl.loop(0, blocks // FETCH)
     def _(step):
         @pl.when(step > 0)
         def _():
-            for u in range(UNROLL):
-                fetch(step * UNROLL + u).wait()
+            for u in range(FETCH):
+                fetch(step * FETCH + u).wait()
 
         for r in range(0, tokens, GROUP):
             group = slice(r, r + GROUP)
             base, total, squares = rows[0, group], rows[1, group], rows[3, group]
-            for u in range(UNROLL):
+            for u in range(FETCH):
                 for c in chunks:
-                    start = (step * UNROLL + u) * width + c * LANES
+                    start = (step * FETCH + u) * width + c * LANES
                     center = x[group, pl.ds(pl.multiple_of(start, LANES), LANES)].astype(F32) - base
                     total = total + center
                     squares = squares + center * center
             rows[1, group] = total
             rows[3, group] = squares
-        for k in [step * UNROLL // 2 + u for u in range(UNROLL // 2)]:
-            gain_pass(2 * k + parity[0], k, left, mine, x, gain, rows, rebuilt, sums, normal=False)
 
     shift = row_mean(rows[1], features)
     variance = jnp.maximum(row_mean(rows[3], features) - shift * shift, 0.0)
@@ -136,9 +140,11 @@
         terms = []
         for side, factors in enumerate((mine, theirs)):
             start = (2 * k + (parity[0] ^ side)) * width
-            scaled = factors[k, :rank, :].astype(F32) * gain[:, pl.ds(pl.multiple_of(start, LANES), width)]
-            terms.append(lax.dot_general(factors[k, rank:, :], scaled.astype(BF16), NT, preferred_element_type=F32))
-        return total + (terms[0] + terms[1])
+            scaled = factors[k, :rank, :] * gain[:, pl.ds(pl.multiple_of(start, LANES), width)].astype(BF16)
+            terms.append(scaled)
+        basis = jnp.concatenate([mine[k, rank:, :], theirs[k, rank:, :]], axis=0)
+        both = lax.dot_general(basis, jnp.concatenate(terms, axis=0), NT, preferred_element_type=F32)
+        return total + (both[:rank, :rank] + both[rank:, rank:])
 
     mixed = lax.fori_loop(0, half, mixing, jnp.zeros((rank, rank), F32), unroll=UNROLL)
     near = lax.dot_general(mixed, mixed, NT, **EXACT)

time: 82.8 us -> 79.8 us (0.964)
  Pallas kernels: 16.9 us -> 13.7 us
    pallas_call x1, Pallas kernels: 7.87 us -> 5.95 us  [on_device(): pl.pallas_call(second_kernel, out_shape=(shape((rank, tokens), F32), shap...]
    pallas_call x1, Pallas kernels: 4.51 us -> 3.42 us  [on_device(): pl.pallas_call(first_kernel, out_shape=(shape((tokens, features), BF16),...]
  transfers between devices with their start and end apart: 3 -> 3, of which waited for: 2 -> 2; matrix products, arithmetic and copies ran while one was open for 0% -> 0% of each run, Pallas kernels for 6% -> 5%
where the time goes in v5:
time: 79.8 us; the launch traced here: 78.3 us
  blocking collectives  45.6 us (57%)
  Pallas kernels  13.7 us (17%)
  waiting for transfers between devices  9.52 us (12%)
  starting transfers between devices  7.58 us (9%)
  other arithmetic  0.96 us (1%)
    all_to_all x1, blocking collectives, on_device(): lax.all_to_all(copies, 'dp', 0, 0, tiled=True, axis_index_groups=groups)  27.5 us
    all_to_all x1, blocking collectives, on_device(): lax.all_to_all(payload, 'dp', 0, 0, tiled=True, axis_index_groups=groups)  18.1 us
    ppermute x1, waiting for transfers between devices, on_device(): lax.ppermute(moved, 'section', [(i, i - 1) for i in range(1, sections)])  7.71 us
    pallas_call x1, Pallas kernels, on_device(): pl.pallas_call(second_kernel, out_shape=(shape((rank, tokens), F32), shap...  5.95 us
    pallas_call x1, Pallas kernels, on_device(): pl.pallas_call(first_kernel, out_shape=(shape((tokens, features), BF16),...  3.42 us
    ppermute x1, starting transfers between devices, on_device(): lax.ppermute(moved, 'section', [(i, i - 1) for i in range(1, sections)])  3.24 us
    pallas_call x1, Pallas kernels, on_device(): pl.pallas_call(lambda *refs: post_kernel(factor, *refs), out_shape=(shape...  3.06 us
    ppermute x1, starting transfers between devices, on_device(): other = lax.ppermute(send, 'dp', others)  2.43 us
  transfers between devices with their start and end apart: 3, of which 2 were waited for; matrix products, arithmetic and copies ran while one was open for 0% of the time, Pallas kernels for 5%

profile of v5, /device:TPU:56, one launch (start us, length us, event | category | flops | bytes accessed | tf_op | source)
XLA Modules:
  0.0 78.3 jit_solution(11459859588867331060)
XLA Ops:
  0.6 1.0 %pad_maximum_fusion = bf16[128,768]{1,0:T(8,128)(2,1)S(1)} fusion(bf16[64,768]{1,0:T(8,128)(2,1)} %bitcast.19, bf16[64,768]{1,0:T(8,128)(2,1)} %bitcast.20), kind=kLoop, calls=%fused_computation | loop fusion | flops 393216 | bytes 393216 | tf_op jit(solution)/shard_map/concatenate | solution.py:356
  1.6 0.1 broadcast_in_dim.12
  1.7 0.0 copy-start
  1.7 0.0 copy-start.1
  1.7 27.5 %all_to_all.10.mine = bf16[8,128,768]{2,1,0:T(8,128)(2,1)S(1)} all-to-all(bf16[8,128,768]{2,1,0:T(8,128)(2,1)S(1)} %broadcast_in_dim.12), channel_id=1, replica_groups={{0,2,4,6,8,10,12,14},{1,3,5,7,9,11,13,15},{16,18,20,22,24,26,28,30},{17..., dimensions={0} | all-to-all | bytes 3145728 | tf_op jit(solution)/shard_map/all_to_all | solution.py:358
  29.2 1.9 %collective-permute-start = (bf16[8,128,768]{2,1,0:T(8,128)(2,1)S(1)}, bf16[8,128,768]{2,1,0:T(8,128)(2,1)S(1)}, u32[]{:S(2)}, u32[]{:S(2)}) collective-permute-start(bf16[8,128,768]{2,1,0:T(8,128)(2,1)S(1)} %all_to_all.10.mine), channel_id=1, source_target_pairs={{0,1},{1,0},{2,3},{3,2},{4,5},{5,4},{6,7},{7,6},{8,9},{9,8},{10,11... | collective-permute-start | bytes 4718600 | tf_op jit(solution)/shard_map/ppermute | solution.py:359
  31.2 0.0 copy-done
  31.2 0.0 copy-done.1
  31.2 3.4 %shard_map.84 = (bf16[128,12288]{1,0:T(8,128)(2,1)S(1)}, bf16[128,64]{1,0:T(8,128)(2,1)S(1)}, f32[4,128,128]{2,1,0:T(8,128)S(1)}, f32[8,128,768]{2,1,0:T(8,128)S(1)}, f32[8,8,768]{2,1,0:T(8,128)S(1)}) custom-call(s32[1]{0:T(128)} %bitcast.parity, bf16[128,12288]{1,0:T(8,128)(2,1)} %bitcast.18, f32[1,12288]{1,0:T(1,128)S(1)} %copy-done, ...), custom_call_target="tpu_custom_call" | custom-call | bytes 25165824 | tf_op jit(solution)/shard_map/pallas_call | solution.py:361
  34.6 0.0 collective-permute-done.theirs
  34.6 5.9 %shard_map.85 = (f32[64,128]{1,0:T(8,128)S(1)}, bf16[8,128,768]{2,1,0:T(8,128)(2,1)S(1)}, f32[8,768]{1,0:T(8,128)S(1)}, bf16[8,80,768]{2,1,0:T(8,128)(2,1)S(1)}) custom-call(s32[1]{0:T(128)} %bitcast.parity, bf16[128,12288]{1,0:T(8,128)(2,1)S(1)} %get-tuple-element.18.x, f32[1,12288]{1,0:T(1,128)S(1)} %copy-done, ...), custom_call_target="tpu_custom_call" | custom-call | tf_op jit(solution)/shard_map/pallas_call | solution.py:376
  40.6 2.4 %collective-permute-start.1 = (bf16[8,80,768]{2,1,0:T(8,128)(2,1)S(1)}, bf16[8,80,768]{2,1,0:T(8,128)(2,1)S(1)}, u32[]{:S(2)}, u32[]{:S(2)}) collective-permute-start(bf16[8,80,768]{2,1,0:T(8,128)(2,1)S(1)} %get-tuple-element.26), channel_id=1, source_target_pairs={{0,1},{1,0},{2,3},{3,2},{4,5},{5,4},{6,7},{7,6},{8,9},{9,8},{10,11... | collective-permute-start | bytes 2949128 | tf_op jit(solution)/shard_map/ppermute | solution.py:395
  43.0 0.4 shard_map.86.keep
  43.4 1.8 %collective-permute-done.1.other = bf16[8,80,768]{2,1,0:T(8,128)(2,1)S(1)} collective-permute-done((bf16[8,80,768]{2,1,0:T(8,128)(2,1)S(1)}, bf16[8,80,768]{2,1,0:T(8,128)(2,1)S(1)}, u32[]{:S(2)}, u32[]{:S(2)}) %collective-permute-start.1) | collective-permute-done | bytes 983072 | tf_op jit(solution)/shard_map/ppermute | solution.py:395
  45.2 0.3 shard_map.87
  45.5 18.1 %all_to_all.11.refs_0_ = bf16[8,80,768]{2,1,0:T(8,128)(2,1)S(1)} all-to-all(bf16[8,80,768]{2,1,0:T(8,128)(2,1)S(1)} %shard_map.87), channel_id=1, replica_groups={{0,2,4,6,8,10,12,14},{1,3,5,7,9,11,13,15},{16,18,20,22,24,26,28,30},{17..., dimensions={0} | all-to-all | bytes 1966080 | tf_op jit(solution)/shard_map/all_to_all | solution.py:412
  63.6 3.1 %shard_map.88 = (f32[1,768]{1,0:T(1,128)}, f32[1,768]{1,0:T(1,128)}, bf16[64,896]{1,0:T(8,128)(2,1)S(1)}) custom-call(bf16[8,80,768]{2,1,0:T(8,128)(2,1)S(1)} %all_to_all.11.refs_0_, f32[64,128]{1,0:T(8,128)S(1)} %get-tuple-element.22.power_t.refs_1_), custom_call_target="tpu_custom_call" | custom-call | tf_op jit(solution)/shard_map/pallas_call | solution.py:415
  66.7 3.2 %collective-permute-start.2 = (bf16[64,896]{1,0:T(8,128)(2,1)S(1)}, bf16[64,896]{1,0:T(8,128)(2,1)S(1)}, u32[]{:S(2)}, u32[]{:S(2)}) collective-permute-start(bf16[64,896]{1,0:T(8,128)(2,1)S(1)} %get-tuple-element.29), channel_id=1, source_target_pairs={{16,0},{32,16},{48,32},{64,48},{80,64},{96,80},{112,96},{128,112},... | collective-permute-start | bytes 344072 | tf_op jit(solution)/shard_map/ppermute | solution.py:424
  69.9 7.7 %collective-permute-done.2.moved = bf16[64,896]{1,0:T(8,128)(2,1)S(1)} collective-permute-done((bf16[64,896]{1,0:T(8,128)(2,1)S(1)}, bf16[64,896]{1,0:T(8,128)(2,1)S(1)}, u32[]{:S(2)}, u32[]{:S(2)}) %collective-permute-start.2) | collective-permute-done | bytes 114720 | tf_op jit(solution)/shard_map/ppermute | solution.py:424
  77.6 0.7 shard_map.89
Async XLA Ops:
  1.7 29.5 %copy-start = (f32[1,12288]{1,0:T(1,128)S(1)}, f32[1,12288]{1,0:T(1,128)}, u32[]{:S(2)}) copy-start(f32[1,12288]{1,0:T(1,128)} %gain.3) | copy-start | bytes 147460
  1.7 29.5 %copy-start.1 = (bf16[1,128,64]{1,2,0:T(8,128)(2,1)S(1)}, bf16[1,128,64]{1,2,0:T(8,128)(2,1)}, u32[]{:S(2)}) copy-start(bf16[1,128,64]{1,2,0:T(8,128)(2,1)} %param.7) | copy-start | bytes 49156
  29.2 5.4 %collective-permute-start = (bf16[8,128,768]{2,1,0:T(8,128)(2,1)S(1)}, bf16[8,128,768]{2,1,0:T(8,128)(2,1)S(1)}, u32[]{:S(2)}, u32[]{:S(2)}) collective-permute-start(bf16[8,128,768]{2,1,0:T(8,128)(2,1)S(1)} %all_to_all.10.mine), channel_id=1, source_target_pairs={{0,1},{1,0},{2,3},{3,2},{4,5},{5,4},{6,7},{7,6},{8,9},{9,8},{10,11... | collective-permute-start | bytes 4718600 | tf_op jit(solution)/shard_map/ppermute | solution.py:359
  40.6 4.6 %collective-permute-start.1 = (bf16[8,80,768]{2,1,0:T(8,128)(2,1)S(1)}, bf16[8,80,768]{2,1,0:T(8,128)(2,1)S(1)}, u32[]{:S(2)}, u32[]{:S(2)}) collective-permute-start(bf16[8,80,768]{2,1,0:T(8,128)(2,1)S(1)} %get-tuple-element.26), channel_id=1, source_target_pairs={{0,1},{1,0},{2,3},{3,2},{4,5},{5,4},{6,7},{7,6},{8,9},{9,8},{10,11... | collective-permute-start | bytes 2949128 | tf_op jit(solution)/shard_map/ppermute | solution.py:395
  66.7 11.0 %collective-permute-start.2 = (bf16[64,896]{1,0:T(8,128)(2,1)S(1)}, bf16[64,896]{1,0:T(8,128)(2,1)S(1)}, u32[]{:S(2)}, u32[]{:S(2)}) collective-permute-start(bf16[64,896]{1,0:T(8,128)(2,1)S(1)} %get-tuple-element.29), channel_id=1, source_target_pairs={{16,0},{32,16},{48,32},{64,48},{80,64},{96,80},{112,96},{128,112},... | collective-permute-start | bytes 344072 | tf_op jit(solution)/shard_map/ppermute | solution.py:424

commit v6 on v5

--- a/solution.py
+++ b/solution.py
@@ -146,17 +146,16 @@
         both = lax.dot_general(basis, jnp.concatenate(terms, axis=0), NT, preferred_element_type=F32)
         return total + (both[:rank, :rank] + both[rank:, rank:])
 
-    mixed = lax.fori_loop(0, half, mixing, jnp.zeros((rank, rank), F32), unroll=UNROLL)
+    mixed = jnp.zeros((rank, rank), F32)
+    for k in range(half):
+        mixed = mixing(k, mixed)
+        gain_pass(2 * k + (1 - parity[0]), k, left, theirs, x, gain, rows, rebuilt, sums)
     near = lax.dot_general(mixed, mixed, NT, **EXACT)
     row = lax.broadcasted_iota(jnp.int32, near.shape, 0)
     col = lax.broadcasted_iota(jnp.int32, near.shape, 1)
     level = jnp.sum(mixed * mixed) * (1e-06 / rank) + 1e-08
-    basis_change = inverse_factor(near + jnp.where(row == col, level, 0.0))
-
-    @pl.loop(0, half // UNROLL)
-    def _(step):
-        for k in [step * UNROLL + u for u in range(UNROLL)]:
-            gain_pass(2 * k + (1 - parity[0]), k, left, theirs, x, gain, rows, rebuilt, sums)
+    lines = []
+    steps = eliminate(near + jnp.where(row == col, level, 0.0), lines)
 
     first = row_mean(rows[2], features)
     second = row_mean(rows[3], features)
@@ -186,8 +185,12 @@
         return step
 
     power = jnp.zeros((tokens, rank), F32)
-    power = lax.fori_loop(0, half, project(0, mine, rebuilt_mine, kept), power, unroll=UNROLL)
-    power = lax.fori_loop(0, half, project(1, theirs, rebuilt, moved), power, unroll=UNROLL)
+    for k in range(half):
+        power = project(0, mine, rebuilt_mine, kept)(k, power)
+        next(steps)
+    for k in range(half):
+        power = project(1, theirs, rebuilt, moved)(k, power)
+    basis_change = jnp.concatenate(lines, axis=0)
     power = lax.dot_general(basis_change, power, NT, **EXACT)
     power_t[...] = power
     pack(lax.dot_general(power, power, NT, **EXACT), packed)
@@ -269,7 +272,7 @@
             out[k, rank:, :] = tail[...].astype(BF16)
 
 
-def inverse_factor(gram):
+def eliminate(gram, done):
     size = gram.shape[0]
     wide = 2 * size
     count = size // 8
@@ -277,35 +280,40 @@
     col = lax.broadcasted_iota(jnp.int32, (size, size), 1)
     work = jnp.concatenate([gram, jnp.where(row == col, 1.0, 0.0).astype(F32)], axis=1)
     parts = [work[8 * i : 8 * i + 8] for i in range(count)]
-    done = []
     for b in range(count):
-        lines = [parts[b][r : r + 1] for r in range(8)]
+        below = range(b + 1, count)
+        lines = [jnp.broadcast_to(parts[b][r : r + 1], (8, wide)) for r in range(8)]
         entry = {
-            (i, j): jnp.broadcast_to(lines[i][:, 8 * b + j : 8 * b + j + 1], (1, wide))
+            (i, j): jnp.broadcast_to(parts[b][i : i + 1, 8 * b + j : 8 * b + j + 1], (8, wide))
             for i in range(8)
             for j in range(i + 1)
         }
-        ratio, scale = {}, []
+        factors = {(i, r): jnp.broadcast_to(parts[i][:, 8 * b + r : 8 * b + r + 1], (8, wide)) for i in below for r in range(8)}
         for r in range(8):
-            scale.append(1.0 / entry[r, r])
-            for i in range(r + 1, 8):
-                ratio[i, r] = entry[i, r] * scale[r]
-            for i in range(r + 1, 8):
-                for j in range(r + 1, i + 1):
-                    entry[i, j] = entry[i, j] - ratio[i, r] * entry[j, r]
-                lines[i] = lines[i] - ratio[i, r] * lines[r]
-        done += [lines[r] * lax.rsqrt(entry[r, r]) for r in range(8)]
-        solved = [None] * 8
-        for r in reversed(range(8)):
-            solved[r] = lines[r] * scale[r]
-            for j in range(r + 1, 8):
-                solved[r] = solved[r] - ratio[j, r] * solved[j]
-        for i in range(b + 1, count):
-            value = parts[i]
-            for r in range(8):
-                value = value - jnp.broadcast_to(parts[i][:, 8 * b + r : 8 * b + r + 1], (8, wide)) * solved[r]
-            parts[i] = value
-    return jnp.concatenate(done, axis=0)[:, size:]
+            scale = 1.0 / entry[r, r]
+            for i in below:
+                factors[i, r] = factors[i, r] * scale
+            for q in range(r + 1, 8):
+                ratio = entry[q, r] * scale
+                for j in range(r + 1, q + 1):
+                    entry[q, j] = entry[q, j] - ratio * entry[j, r]
+                for i in below:
+                    factors[i, q] = factors[i, q] - factors[i, r] * entry[q, r]
+                lines[q] = lines[q] - ratio * lines[r]
+        done += [(lines[r] * lax.rsqrt(entry[r, r]))[:1, size:] for r in range(8)]
+        for i in below:
+            terms = [factors[i, r] * lines[r] for r in range(8)]
+            while len(terms) > 1:
+                terms = [terms[t] + terms[t + 1] for t in range(0, len(terms), 2)]
+            parts[i] = parts[i] - terms[0]
+        yield
+
+
+def inverse_factor(gram):
+    done = []
+    for _ in eliminate(gram, done):
+        pass
+    return jnp.concatenate(done, axis=0)
 
 
 def post_kernel(factor, terms, power_t, gain_out, bias_out, moved, square):
@@ -322,12 +330,10 @@
     moved[:, width:] = jnp.dot(inverse, power_t[...], **EXACT).astype(BF16)
 
 
-def place_kernel(moved, left_out, right_out, sent):
+def place_kernel(moved, gain, bias, left_out, right_out, gain_out, bias_out, sent):
     width = right_out.shape[1]
-    copies = [
-        pltpu.make_async_copy(moved.at[:, :width], right_out, sent.at[0]),
-        pltpu.make_async_copy(moved.at[:, width:], left_out, sent.at[1]),
-    ]
+    pairs = ((moved.at[:, :width], right_out), (moved.at[:, width:], left_out), (gain, gain_out), (bias, bias_out))
+    copies = [pltpu.make_async_copy(source, target, sent.at[i]) for i, (source, target) in enumerate(pairs)]
     for copy in copies:
         copy.start()
     for copy in copies:
@@ -412,7 +418,7 @@
     terms = lax.all_to_all(payload, "dp", 0, 0, tiled=True, axis_index_groups=groups)
 
     factor = float(1.0 / (tokens * replicas) ** 0.5)
-    gain_grad, bias_grad, moved = pl.pallas_call(
+    gain_sums, bias_sums, moved = pl.pallas_call(
         lambda *refs: post_kernel(factor, *refs),
         out_shape=(shape((1, width), F32), shape((1, width), F32), shape((rank, width + tokens), BF16)),
         in_specs=[VMEM, VMEM],
@@ -422,14 +428,14 @@
     )(terms, power_t)
     sections = lax.axis_size("section")
     moved = lax.ppermute(moved, "section", [(i, i - 1) for i in range(1, sections)])
-    left_out, right_out = pl.pallas_call(
+    left_out, right_out, gain_grad, bias_grad = pl.pallas_call(
         place_kernel,
-        out_shape=(shape((rank, tokens), BF16), shape((rank, width), BF16)),
-        in_specs=[VMEM],
-        out_specs=(pl.BlockSpec(memory_space=pltpu.HBM),) * 2,
-        scratch_shapes=[pltpu.SemaphoreType.DMA((2,))],
+        out_shape=(shape((rank, tokens), BF16), shape((rank, width), BF16), shape((1, width), F32), shape((1, width), F32)),
+        in_specs=[VMEM] * 3,
+        out_specs=(pl.BlockSpec(memory_space=pltpu.HBM),) * 4,
+        scratch_shapes=[pltpu.SemaphoreType.DMA((4,))],
         compiler_params=limit(4),
-    )(moved)
+    )(moved, gain_sums, bias_sums)
     return gain_grad, bias_grad, left_out.T[None], right_out.T[None]
 
 

time: 79.8 us -> 78.9 us (0.989)
  Pallas kernels: 13.7 us -> 12.8 us
where the time goes in v6:
time: 78.9 us; the launch traced here: 77.4 us
  blocking collectives  45.6 us (58%)
  Pallas kernels  12.8 us (16%)
  waiting for transfers between devices  9.52 us (12%)
  starting transfers between devices  7.58 us (10%)
  other arithmetic  0.96 us (1%)
    all_to_all x1, blocking collectives, on_device(): lax.all_to_all(copies, 'dp', 0, 0, tiled=True, axis_index_groups=groups)  27.5 us
    all_to_all x1, blocking collectives, on_device(): lax.all_to_all(payload, 'dp', 0, 0, tiled=True, axis_index_groups=groups)  18.1 us
    ppermute x1, waiting for transfers between devices, on_device(): lax.ppermute(moved, 'section', [(i, i - 1) for i in range(1, sections)])  7.71 us
    pallas_call x1, Pallas kernels, on_device(): pl.pallas_call(second_kernel, out_shape=(shape((rank, tokens), F32), shap...  5.75 us
    pallas_call x1, Pallas kernels, on_device(): pl.pallas_call(first_kernel, out_shape=(shape((tokens, features), BF16),...  3.42 us
    ppermute x1, starting transfers between devices, on_device(): lax.ppermute(moved, 'section', [(i, i - 1) for i in range(1, sections)])  3.26 us
    ppermute x1, starting transfers between devices, on_device(): other = lax.ppermute(send, 'dp', others)  2.41 us
    pallas_call x1, Pallas kernels, on_device(): pl.pallas_call(lambda *refs: post_kernel(factor, *refs), out_shape=(shape...  2.35 us
  transfers between devices with their start and end apart: 3, of which 2 were waited for; matrix products, arithmetic and copies ran while one was open for 0% of the time, Pallas kernels for 5%

profile of v6, /device:TPU:56, one launch (start us, length us, event | category | flops | bytes accessed | tf_op | source)
XLA Modules:
  0.0 77.4 jit_solution(8512549406200797847)
XLA Ops:
  0.6 1.0 %pad_maximum_fusion = bf16[128,768]{1,0:T(8,128)(2,1)S(1)} fusion(bf16[64,768]{1,0:T(8,128)(2,1)} %bitcast.19, bf16[64,768]{1,0:T(8,128)(2,1)} %bitcast.20), kind=kLoop, calls=%fused_computation | loop fusion | flops 393216 | bytes 393216 | tf_op jit(solution)/shard_map/concatenate | solution.py:362
  1.6 0.1 broadcast_in_dim.12
  1.7 0.0 copy-start
  1.7 0.0 copy-start.1
  1.7 27.5 %all_to_all.10.mine = bf16[8,128,768]{2,1,0:T(8,128)(2,1)S(1)} all-to-all(bf16[8,128,768]{2,1,0:T(8,128)(2,1)S(1)} %broadcast_in_dim.12), channel_id=1, replica_groups={{0,2,4,6,8,10,12,14},{1,3,5,7,9,11,13,15},{16,18,20,22,24,26,28,30},{17..., dimensions={0} | all-to-all | bytes 3145728 | tf_op jit(solution)/shard_map/all_to_all | solution.py:364
  29.2 1.9 %collective-permute-start = (bf16[8,128,768]{2,1,0:T(8,128)(2,1)S(1)}, bf16[8,128,768]{2,1,0:T(8,128)(2,1)S(1)}, u32[]{:S(2)}, u32[]{:S(2)}) collective-permute-start(bf16[8,128,768]{2,1,0:T(8,128)(2,1)S(1)} %all_to_all.10.mine), channel_id=1, source_target_pairs={{0,1},{1,0},{2,3},{3,2},{4,5},{5,4},{6,7},{7,6},{8,9},{9,8},{10,11... | collective-permute-start | bytes 4718600 | tf_op jit(solution)/shard_map/ppermute | solution.py:365
  31.2 0.0 copy-done
  31.2 0.0 copy-done.1
  31.2 3.4 %shard_map.84 = (bf16[128,12288]{1,0:T(8,128)(2,1)S(1)}, bf16[128,64]{1,0:T(8,128)(2,1)S(1)}, f32[4,128,128]{2,1,0:T(8,128)S(1)}, f32[8,128,768]{2,1,0:T(8,128)S(1)}, f32[8,8,768]{2,1,0:T(8,128)S(1)}) custom-call(s32[1]{0:T(128)} %bitcast.parity, bf16[128,12288]{1,0:T(8,128)(2,1)} %bitcast.18, f32[1,12288]{1,0:T(1,128)S(1)} %copy-done, ...), custom_call_target="tpu_custom_call" | custom-call | bytes 25165824 | tf_op jit(solution)/shard_map/pallas_call | solution.py:367
  34.6 0.0 collective-permute-done.theirs
  34.6 5.8 %shard_map.85 = (f32[64,128]{1,0:T(8,128)S(1)}, bf16[8,128,768]{2,1,0:T(8,128)(2,1)S(1)}, f32[8,768]{1,0:T(8,128)S(1)}, bf16[8,80,768]{2,1,0:T(8,128)(2,1)S(1)}) custom-call(s32[1]{0:T(128)} %bitcast.parity, bf16[128,12288]{1,0:T(8,128)(2,1)S(1)} %get-tuple-element.20.x, f32[1,12288]{1,0:T(1,128)S(1)} %copy-done, ...), custom_call_target="tpu_custom_call" | custom-call | tf_op jit(solution)/shard_map/pallas_call | solution.py:382
  40.4 2.4 %collective-permute-start.1 = (bf16[8,80,768]{2,1,0:T(8,128)(2,1)S(1)}, bf16[8,80,768]{2,1,0:T(8,128)(2,1)S(1)}, u32[]{:S(2)}, u32[]{:S(2)}) collective-permute-start(bf16[8,80,768]{2,1,0:T(8,128)(2,1)S(1)} %get-tuple-element.28), channel_id=1, source_target_pairs={{0,1},{1,0},{2,3},{3,2},{4,5},{5,4},{6,7},{7,6},{8,9},{9,8},{10,11... | collective-permute-start | bytes 2949128 | tf_op jit(solution)/shard_map/ppermute | solution.py:401
  42.8 0.4 shard_map.86.keep
  43.2 1.8 %collective-permute-done.1.other = bf16[8,80,768]{2,1,0:T(8,128)(2,1)S(1)} collective-permute-done((bf16[8,80,768]{2,1,0:T(8,128)(2,1)S(1)}, bf16[8,80,768]{2,1,0:T(8,128)(2,1)S(1)}, u32[]{:S(2)}, u32[]{:S(2)}) %collective-permute-start.1) | collective-permute-done | bytes 983072 | tf_op jit(solution)/shard_map/ppermute | solution.py:401
  45.0 0.3 shard_map.87
  45.3 18.1 %all_to_all.11.refs_0_ = bf16[8,80,768]{2,1,0:T(8,128)(2,1)S(1)} all-to-all(bf16[8,80,768]{2,1,0:T(8,128)(2,1)S(1)} %shard_map.87), channel_id=1, replica_groups={{0,2,4,6,8,10,12,14},{1,3,5,7,9,11,13,15},{16,18,20,22,24,26,28,30},{17..., dimensions={0} | all-to-all | bytes 1966080 | tf_op jit(solution)/shard_map/all_to_all | solution.py:418
  63.4 2.3 %shard_map.88 = (f32[1,768]{1,0:T(1,128)S(1)}, f32[1,768]{1,0:T(1,128)S(1)}, bf16[64,896]{1,0:T(8,128)(2,1)S(1)}) custom-call(bf16[8,80,768]{2,1,0:T(8,128)(2,1)S(1)} %all_to_all.11.refs_0_, f32[64,128]{1,0:T(8,128)S(1)} %get-tuple-element.24.power_t.refs_1_), custom_call_target="tpu_custom_call" | custom-call | tf_op jit(solution)/shard_map/pallas_call | solution.py:421
  65.7 3.3 %collective-permute-start.2 = (bf16[64,896]{1,0:T(8,128)(2,1)S(1)}, bf16[64,896]{1,0:T(8,128)(2,1)S(1)}, u32[]{:S(2)}, u32[]{:S(2)}) collective-permute-start(bf16[64,896]{1,0:T(8,128)(2,1)S(1)} %get-tuple-element.29), channel_id=1, source_target_pairs={{16,0},{32,16},{48,32},{64,48},{80,64},{96,80},{112,96},{128,112},... | collective-permute-start | bytes 344072 | tf_op jit(solution)/shard_map/ppermute | solution.py:430
  69.0 7.7 %collective-permute-done.2.moved = bf16[64,896]{1,0:T(8,128)(2,1)S(1)} collective-permute-done((bf16[64,896]{1,0:T(8,128)(2,1)S(1)}, bf16[64,896]{1,0:T(8,128)(2,1)S(1)}, u32[]{:S(2)}, u32[]{:S(2)}) %collective-permute-start.2) | collective-permute-done | bytes 114720 | tf_op jit(solution)/shard_map/ppermute | solution.py:430
  76.7 0.7 shard_map.89
Async XLA Ops:
  1.7 29.5 %copy-start = (f32[1,12288]{1,0:T(1,128)S(1)}, f32[1,12288]{1,0:T(1,128)}, u32[]{:S(2)}) copy-start(f32[1,12288]{1,0:T(1,128)} %gain.3) | copy-start | bytes 147460
  1.7 29.5 %copy-start.1 = (bf16[1,128,64]{1,2,0:T(8,128)(2,1)S(1)}, bf16[1,128,64]{1,2,0:T(8,128)(2,1)}, u32[]{:S(2)}) copy-start(bf16[1,128,64]{1,2,0:T(8,128)(2,1)} %param.7) | copy-start | bytes 49156
  29.2 5.4 %collective-permute-start = (bf16[8,128,768]{2,1,0:T(8,128)(2,1)S(1)}, bf16[8,128,768]{2,1,0:T(8,128)(2,1)S(1)}, u32[]{:S(2)}, u32[]{:S(2)}) collective-permute-start(bf16[8,128,768]{2,1,0:T(8,128)(2,1)S(1)} %all_to_all.10.mine), channel_id=1, source_target_pairs={{0,1},{1,0},{2,3},{3,2},{4,5},{5,4},{6,7},{7,6},{8,9},{9,8},{10,11... | collective-permute-start | bytes 4718600 | tf_op jit(solution)/shard_map/ppermute | solution.py:365
  40.4 4.6 %collective-permute-start.1 = (bf16[8,80,768]{2,1,0:T(8,128)(2,1)S(1)}, bf16[8,80,768]{2,1,0:T(8,128)(2,1)S(1)}, u32[]{:S(2)}, u32[]{:S(2)}) collective-permute-start(bf16[8,80,768]{2,1,0:T(8,128)(2,1)S(1)} %get-tuple-element.28), channel_id=1, source_target_pairs={{0,1},{1,0},{2,3},{3,2},{4,5},{5,4},{6,7},{7,6},{8,9},{9,8},{10,11... | collective-permute-start | bytes 2949128 | tf_op jit(solution)/shard_map/ppermute | solution.py:401
  65.7 11.0 %collective-permute-start.2 = (bf16[64,896]{1,0:T(8,128)(2,1)S(1)}, bf16[64,896]{1,0:T(8,128)(2,1)S(1)}, u32[]{:S(2)}, u32[]{:S(2)}) collective-permute-start(bf16[64,896]{1,0:T(8,128)(2,1)S(1)} %get-tuple-element.29), channel_id=1, source_target_pairs={{16,0},{32,16},{48,32},{64,48},{80,64},{96,80},{112,96},{128,112},... | collective-permute-start | bytes 344072 | tf_op jit(solution)/shard_map/ppermute | solution.py:430

commit v7 on v6

--- a/solution.py
+++ b/solution.py
@@ -63,6 +63,25 @@
     return jnp.broadcast_to(jnp.sum(total, axis=1, keepdims=True) * (1.0 / features), total.shape)
 
 
+def copies_kernel(left_t, right_t, basis_t, copies, left, packed, arrived):
+    rank = left_t.shape[0]
+    own = copies.at[0]
+    fetches = [
+        pltpu.make_async_copy(left_t, left, arrived.at[0]),
+        pltpu.make_async_copy(right_t, own.at[:rank, :], arrived.at[1]),
+        pltpu.make_async_copy(basis_t, own.at[rank : 2 * rank, :], arrived.at[2]),
+    ]
+    for fetch in fetches:
+        fetch.start()
+    fetches[0].wait()
+    pack(lax.dot_general(left[...], left[...], NT, preferred_element_type=F32), packed)
+    copies[0, 2 * rank :, :] = jnp.concatenate(split(packed[0:4, :], 2), axis=0).astype(BF16)
+    for fetch in fetches[1:]:
+        fetch.wait()
+    for k in range(1, copies.shape[0]):
+        copies[k] = copies[0]
+
+
 def first_kernel(parity, x_hbm, gain, left_t, mine, x, left_out, rows, rebuilt, sums, arrived):
     half, _, width = mine.shape
     tokens, features = x.shape
@@ -127,7 +146,7 @@
 
 
 def second_kernel(
-    parity, x, gain, left_ref, rows_in, rebuilt_mine, mine, theirs, power_t, kept, packed, send, rows, rebuilt, sums, moved, tail
+    parity, x, gain, left_ref, rows_in, rebuilt_mine, mine, theirs, power_t, kept, packed, send, rows, rebuilt, sums, moved, tail, square
 ):
     half, height, width = theirs.shape
     tokens, features = x.shape
@@ -136,26 +155,38 @@
     left = left_ref[...]
     rows[...] = rows_in[...]
 
-    def mixing(k, total):
+    ones = jnp.ones((GROUP, width), BF16)
+
+    def mixing(k, totals):
         terms = []
         for side, factors in enumerate((mine, theirs)):
             start = (2 * k + (parity[0] ^ side)) * width
-            scaled = factors[k, :rank, :] * gain[:, pl.ds(pl.multiple_of(start, LANES), width)].astype(BF16)
-            terms.append(scaled)
-        basis = jnp.concatenate([mine[k, rank:, :], theirs[k, rank:, :]], axis=0)
-        both = lax.dot_general(basis, jnp.concatenate(terms, axis=0), NT, preferred_element_type=F32)
-        return total + (both[:rank, :rank] + both[rank:, rank:])
-
-    mixed = jnp.zeros((rank, rank), F32)
+            terms.append(factors[k, :rank, :] * gain[:, pl.ds(pl.multiple_of(start, LANES), width)].astype(BF16))
+        basis = jnp.concatenate([mine[k, rank : 2 * rank, :], theirs[k, rank : 2 * rank, :], ones], axis=0)
+        both = lax.dot_general(basis, jnp.concatenate(terms + [ones], axis=0), NT, preferred_element_type=F32)
+        near, far = slice(0, rank), slice(rank, 2 * rank)
+        last = slice(2 * rank, 2 * rank + 1)
+        spread = [factors[k, 2 * rank :, :].astype(F32) for factors in (mine, theirs)]
+        values = (
+            both[near, near] + both[far, far],
+            both[near, last] + both[far, last],
+            both[last, near] + both[last, far],
+            spread[0] + spread[1],
+        )
+        return tuple(total + value for total, value in zip(totals, values))
+
+    totals = (jnp.zeros((rank, rank), F32), jnp.zeros((rank, 1), F32), jnp.zeros((1, rank), F32), jnp.zeros((8, width), F32))
     for k in range(half):
-        mixed = mixing(k, mixed)
+        totals = mixing(k, totals)
         gain_pass(2 * k + (1 - parity[0]), k, left, theirs, x, gain, rows, rebuilt, sums)
-    near = lax.dot_general(mixed, mixed, NT, **EXACT)
+    mixed = totals[0] - totals[1] * (totals[2] * (1.0 / features))
+    spread = unpack(totals[3][0:4] + totals[3][4:8], square) * (1.0 / (2 * half * tokens))
+    near = lax.dot_general(jnp.dot(mixed, spread, **EXACT), mixed, NT, **EXACT)
     row = lax.broadcasted_iota(jnp.int32, near.shape, 0)
     col = lax.broadcasted_iota(jnp.int32, near.shape, 1)
-    level = jnp.sum(mixed * mixed) * (1e-06 / rank) + 1e-08
+    level = jnp.sum(jnp.where(row == col, near, 0.0)) * 1e-05 + 1e-08
     lines = []
-    steps = eliminate(near + jnp.where(row == col, level, 0.0), lines)
+    steps = eliminate(near + jnp.where(row == col, level, 0.0), lines, 0.25 * level)
 
     first = row_mean(rows[2], features)
     second = row_mean(rows[3], features)
@@ -180,7 +211,7 @@
                     target[k, group, lanes] = values[-1]
                 groups.append(jnp.concatenate(values, axis=1))
             block = jnp.concatenate(groups, axis=0)
-            return total + lax.dot_general(block, factors[k, rank:, :], NT, preferred_element_type=F32)
+            return total + lax.dot_general(block, factors[k, rank : 2 * rank, :], NT, preferred_element_type=F32)
 
         return step
 
@@ -272,7 +303,7 @@
             out[k, rank:, :] = tail[...].astype(BF16)
 
 
-def eliminate(gram, done):
+def eliminate(gram, done, floor=None):
     size = gram.shape[0]
     wide = 2 * size
     count = size // 8
@@ -290,6 +321,8 @@
         }
         factors = {(i, r): jnp.broadcast_to(parts[i][:, 8 * b + r : 8 * b + r + 1], (8, wide)) for i in below for r in range(8)}
         for r in range(8):
+            if floor is not None:
+                entry[r, r] = jnp.maximum(entry[r, r], floor)
             scale = 1.0 / entry[r, r]
             for i in below:
                 factors[i, r] = factors[i, r] * scale
@@ -359,8 +392,15 @@
     shape = jax.ShapeDtypeStruct
 
     x_hbm = pltpu.with_memory_space_constraint(saved_input[0], pltpu.HBM)
-    own = jnp.concatenate([right_in[0].T, basis[0].T], axis=0)
-    copies = jnp.broadcast_to(own[None], (half,) + own.shape)
+    own = [pltpu.with_memory_space_constraint(factor[0].T, pltpu.HBM) for factor in (left_in, right_in, basis)]
+    copies = pl.pallas_call(
+        copies_kernel,
+        out_shape=shape((half, 2 * rank + 8, width), BF16),
+        in_specs=[pl.BlockSpec(memory_space=pltpu.HBM)] * 3,
+        out_specs=VMEM,
+        scratch_shapes=[pltpu.VMEM((rank, tokens), BF16), pltpu.VMEM((8, width), F32), pltpu.SemaphoreType.DMA((3,))],
+        compiler_params=limit(4),
+    )(*own)
     mine = lax.all_to_all(copies, "dp", 0, 0, tiled=True, axis_index_groups=groups)
     theirs = lax.ppermute(mine, "dp", others)
     parity = (lax.axis_index("dp") & 1).astype(jnp.int32).reshape(1)
@@ -395,6 +435,7 @@
             pltpu.VMEM((half, 8, width), F32),
             pltpu.VMEM((half, tokens, width), BF16),
             pltpu.VMEM((16, width), F32),
+            pltpu.VMEM((24, LANES), F32),
         ],
         compiler_params=limit(32),
     )(parity, x, norm_gain, left, rows, rebuilt, mine, theirs)

time: 78.9 us -> 80.9 us (1.025)
  Pallas kernels: 12.8 us -> 14.7 us
  blocking collectives: 45.6 us -> 46.8 us
  other arithmetic: 0.96 us -> 0 us
    all_to_all x1, blocking collectives: 27.5 us -> 28.7 us  [on_device(): lax.all_to_all(copies, 'dp', 0, 0, tiled=True, axis_index_groups=groups)]
    pallas_call x0 -> x1, Pallas kernels: none -> 1.08 us  [on_device(): pl.pallas_call(copies_kernel, out_shape=shape((half, 2 * rank + 8, width)...]
    concatenate x1 -> x0, other arithmetic: 0.96 us -> none  [on_device(): own = jnp.concatenate([right_in[0].T, basis[0].T], axis=0)]
    pallas_call x1, Pallas kernels: 5.75 us -> 6.57 us  [on_device(): pl.pallas_call(second_kernel, out_shape=(shape((rank, tokens), F32), shap...]
  transfers between devices with their start and end apart: 3 -> 3, of which waited for: 2 -> 3; matrix products, arithmetic and copies ran while one was open for 0% -> 0% of each run, Pallas kernels for 5% -> 5%
where the time goes in v7:
time: 80.9 us; the launch traced here: 79.4 us
  blocking collectives  46.8 us (58%)
  Pallas kernels  14.7 us (18%)
  waiting for transfers between devices  9.59 us (12%)
  starting transfers between devices  7.52 us (9%)
    all_to_all x1, blocking collectives, on_device(): lax.all_to_all(copies, 'dp', 0, 0, tiled=True, axis_index_groups=groups)  28.7 us
    all_to_all x1, blocking collectives, on_device(): lax.all_to_all(payload, 'dp', 0, 0, tiled=True, axis_index_groups=groups)  18.1 us
    ppermute x1, waiting for transfers between devices, on_device(): lax.ppermute(moved, 'section', [(i, i - 1) for i in range(1, sections)])  7.72 us
    pallas_call x1, Pallas kernels, on_device(): pl.pallas_call(second_kernel, out_shape=(shape((rank, tokens), F32), shap...  6.57 us
    pallas_call x1, Pallas kernels, on_device(): pl.pallas_call(first_kernel, out_shape=(shape((tokens, features), BF16),...  3.42 us
    ppermute x1, starting transfers between devices, on_device(): lax.ppermute(moved, 'section', [(i, i - 1) for i in range(1, sections)])  3.25 us
    ppermute x1, starting transfers between devices, on_device(): other = lax.ppermute(send, 'dp', others)  2.36 us
    pallas_call x1, Pallas kernels, on_device(): pl.pallas_call(lambda *refs: post_kernel(factor, *refs), out_shape=(shape...  2.34 us
  transfers between devices with their start and end apart: 3, of which 3 were waited for; matrix products, arithmetic and copies ran while one was open for 0% of the time, Pallas kernels for 5%

profile of v7, /device:TPU:56, one launch (start us, length us, event | category | flops | bytes accessed | tf_op | source)
XLA Modules:
  0.0 79.4 jit_solution(11834516451270618338)
XLA Ops:
  0.6 1.1 %shard_map.84 = bf16[8,136,768]{2,1,0:T(8,128)(2,1)S(1)} custom-call(bf16[64,128]{1,0:T(8,128)(2,1)} %bitcast.17, bf16[64,768]{1,0:T(8,128)(2,1)} %bitcast.20, bf16[64,768]{1,0:T(8,128)(2,1)} %bitcast.21), custom_call_target="tpu_custom_call" | custom-call | tf_op jit(solution)/shard_map/pallas_call | solution.py:396
  1.7 0.0 copy-start
  1.7 0.0 copy-start.1
  1.7 28.7 %all_to_all.10.mine = bf16[8,136,768]{2,1,0:T(8,128)(2,1)S(1)} all-to-all(bf16[8,136,768]{2,1,0:T(8,128)(2,1)S(1)} %shard_map.84), channel_id=1, replica_groups={{0,2,4,6,8,10,12,14},{1,3,5,7,9,11,13,15},{16,18,20,22,24,26,28,30},{17..., dimensions={0} | all-to-all | bytes 3342336 | tf_op jit(solution)/shard_map/all_to_all | solution.py:404
  30.4 1.9 %collective-permute-start = (bf16[8,136,768]{2,1,0:T(8,128)(2,1)S(1)}, bf16[8,136,768]{2,1,0:T(8,128)(2,1)S(1)}, u32[]{:S(2)}, u32[]{:S(2)}) collective-permute-start(bf16[8,136,768]{2,1,0:T(8,128)(2,1)S(1)} %all_to_all.10.mine), channel_id=1, source_target_pairs={{0,1},{1,0},{2,3},{3,2},{4,5},{5,4},{6,7},{7,6},{8,9},{9,8},{10,11... | collective-permute-start | bytes 5013512 | tf_op jit(solution)/shard_map/ppermute | solution.py:405
  32.3 0.0 copy-done
  32.3 0.0 copy-done.1
  32.3 3.4 %shard_map.85 = (bf16[128,12288]{1,0:T(8,128)(2,1)S(1)}, bf16[128,64]{1,0:T(8,128)(2,1)S(1)}, f32[4,128,128]{2,1,0:T(8,128)S(1)}, f32[8,128,768]{2,1,0:T(8,128)S(1)}, f32[8,8,768]{2,1,0:T(8,128)S(1)}) custom-call(s32[1]{0:T(128)} %bitcast.parity, bf16[128,12288]{1,0:T(8,128)(2,1)} %bitcast.19, f32[1,12288]{1,0:T(1,128)S(1)} %copy-done, ...), custom_call_target="tpu_custom_call" | custom-call | bytes 25165824 | tf_op jit(solution)/shard_map/pallas_call | solution.py:407
  35.8 0.1 collective-permute-done.theirs
  35.8 6.6 %shard_map.86 = (f32[64,128]{1,0:T(8,128)S(1)}, bf16[8,128,768]{2,1,0:T(8,128)(2,1)S(1)}, f32[8,768]{1,0:T(8,128)S(1)}, bf16[8,80,768]{2,1,0:T(8,128)(2,1)S(1)}) custom-call(s32[1]{0:T(128)} %bitcast.parity, bf16[128,12288]{1,0:T(8,128)(2,1)S(1)} %get-tuple-element.20.x, f32[1,12288]{1,0:T(1,128)S(1)} %copy-done, ...), custom_call_target="tpu_custom_call" | custom-call | tf_op jit(solution)/shard_map/pallas_call | solution.py:422
  42.4 2.4 %collective-permute-start.1 = (bf16[8,80,768]{2,1,0:T(8,128)(2,1)S(1)}, bf16[8,80,768]{2,1,0:T(8,128)(2,1)S(1)}, u32[]{:S(2)}, u32[]{:S(2)}) collective-permute-start(bf16[8,80,768]{2,1,0:T(8,128)(2,1)S(1)} %get-tuple-element.28), channel_id=1, source_target_pairs={{0,1},{1,0},{2,3},{3,2},{4,5},{5,4},{6,7},{7,6},{8,9},{9,8},{10,11... | collective-permute-start | bytes 2949128 | tf_op jit(solution)/shard_map/ppermute | solution.py:442
  44.8 0.4 shard_map.87.keep
  45.1 1.8 %collective-permute-done.1.other = bf16[8,80,768]{2,1,0:T(8,128)(2,1)S(1)} collective-permute-done((bf16[8,80,768]{2,1,0:T(8,128)(2,1)S(1)}, bf16[8,80,768]{2,1,0:T(8,128)(2,1)S(1)}, u32[]{:S(2)}, u32[]{:S(2)}) %collective-permute-start.1) | collective-permute-done | bytes 983072 | tf_op jit(solution)/shard_map/ppermute | solution.py:442
  47.0 0.3 shard_map.88
  47.2 18.1 %all_to_all.11.refs_0_ = bf16[8,80,768]{2,1,0:T(8,128)(2,1)S(1)} all-to-all(bf16[8,80,768]{2,1,0:T(8,128)(2,1)S(1)} %shard_map.88), channel_id=1, replica_groups={{0,2,4,6,8,10,12,14},{1,3,5,7,9,11,13,15},{16,18,20,22,24,26,28,30},{17..., dimensions={0} | all-to-all | bytes 1966080 | tf_op jit(solution)/shard_map/all_to_all | solution.py:459
  65.4 2.3 %shard_map.89 = (f32[1,768]{1,0:T(1,128)S(1)}, f32[1,768]{1,0:T(1,128)S(1)}, bf16[64,896]{1,0:T(8,128)(2,1)S(1)}) custom-call(bf16[8,80,768]{2,1,0:T(8,128)(2,1)S(1)} %all_to_all.11.refs_0_, f32[64,128]{1,0:T(8,128)S(1)} %get-tuple-element.24.power_t.refs_1_), custom_call_target="tpu_custom_call" | custom-call | tf_op jit(solution)/shard_map/pallas_call | solution.py:462
  67.7 3.2 %collective-permute-start.2 = (bf16[64,896]{1,0:T(8,128)(2,1)S(1)}, bf16[64,896]{1,0:T(8,128)(2,1)S(1)}, u32[]{:S(2)}, u32[]{:S(2)}) collective-permute-start(bf16[64,896]{1,0:T(8,128)(2,1)S(1)} %get-tuple-element.29), channel_id=1, source_target_pairs={{16,0},{32,16},{48,32},{64,48},{80,64},{96,80},{112,96},{128,112},... | collective-permute-start | bytes 344072 | tf_op jit(solution)/shard_map/ppermute | solution.py:471
  71.0 7.7 %collective-permute-done.2.moved = bf16[64,896]{1,0:T(8,128)(2,1)S(1)} collective-permute-done((bf16[64,896]{1,0:T(8,128)(2,1)S(1)}, bf16[64,896]{1,0:T(8,128)(2,1)S(1)}, u32[]{:S(2)}, u32[]{:S(2)}) %collective-permute-start.2) | collective-permute-done | bytes 114720 | tf_op jit(solution)/shard_map/ppermute | solution.py:471
  78.7 0.7 shard_map.90
Async XLA Ops:
  1.7 30.6 %copy-start = (f32[1,12288]{1,0:T(1,128)S(1)}, f32[1,12288]{1,0:T(1,128)}, u32[]{:S(2)}) copy-start(f32[1,12288]{1,0:T(1,128)} %gain.3) | copy-start | bytes 147460
  1.7 30.6 %copy-start.1 = (bf16[1,128,64]{1,2,0:T(8,128)(2,1)S(1)}, bf16[1,128,64]{1,2,0:T(8,128)(2,1)}, u32[]{:S(2)}) copy-start(bf16[1,128,64]{1,2,0:T(8,128)(2,1)} %param.7) | copy-start | bytes 49156
  30.4 5.4 %collective-permute-start = (bf16[8,136,768]{2,1,0:T(8,128)(2,1)S(1)}, bf16[8,136,768]{2,1,0:T(8,128)(2,1)S(1)}, u32[]{:S(2)}, u32[]{:S(2)}) collective-permute-start(bf16[8,136,768]{2,1,0:T(8,128)(2,1)S(1)} %all_to_all.10.mine), channel_id=1, source_target_pairs={{0,1},{1,0},{2,3},{3,2},{4,5},{5,4},{6,7},{7,6},{8,9},{9,8},{10,11... | collective-permute-start | bytes 5013512 | tf_op jit(solution)/shard_map/ppermute | solution.py:405
  42.4 4.5 %collective-permute-start.1 = (bf16[8,80,768]{2,1,0:T(8,128)(2,1)S(1)}, bf16[8,80,768]{2,1,0:T(8,128)(2,1)S(1)}, u32[]{:S(2)}, u32[]{:S(2)}) collective-permute-start(bf16[8,80,768]{2,1,0:T(8,128)(2,1)S(1)} %get-tuple-element.28), channel_id=1, source_target_pairs={{0,1},{1,0},{2,3},{3,2},{4,5},{5,4},{6,7},{7,6},{8,9},{9,8},{10,11... | collective-permute-start | bytes 2949128 | tf_op jit(solution)/shard_map/ppermute | solution.py:442
  67.7 11.0 %collective-permute-start.2 = (bf16[64,896]{1,0:T(8,128)(2,1)S(1)}, bf16[64,896]{1,0:T(8,128)(2,1)S(1)}, u32[]{:S(2)}, u32[]{:S(2)}) collective-permute-start(bf16[64,896]{1,0:T(8,128)(2,1)S(1)} %get-tuple-element.29), channel_id=1, source_target_pairs={{16,0},{32,16},{48,32},{64,48},{80,64},{96,80},{112,96},{128,112},... | collective-permute-start | bytes 344072 | tf_op jit(solution)/shard_map/ppermute | solution.py:471

commit v8 on v7

--- a/solution.py
+++ b/solution.py
@@ -47,6 +47,7 @@
                 normed = (x[group, columns[c]].astype(F32) - mean) * inverse
                 second = second + scaled * normed
                 products[c] = products[c] + fold(part * normed)
+                rebuilt[k, group, c * LANES : (c + 1) * LANES] = scaled
         if plain:
             rows[2, group] = first
         if normal:
@@ -197,7 +198,6 @@
         def step(k, total):
             j = 2 * k + (parity[0] ^ side)
             columns = [pl.ds(pl.multiple_of(j * width + c * LANES, LANES), LANES) for c in chunks]
-            gains = [jnp.broadcast_to(gain[:, columns[c]], (GROUP, LANES)) for c in chunks]
             groups = []
             for r in range(0, tokens, GROUP):
                 group = slice(r, r + GROUP)
@@ -205,8 +205,7 @@
                 values = []
                 for c in chunks:
                     lanes = slice(c * LANES, (c + 1) * LANES)
-                    scaled = source[k, group, lanes] * gains[c]
-                    value = scaled * inverse - x[group, columns[c]].astype(F32) * slope + offset
+                    value = source[k, group, lanes] * inverse - x[group, columns[c]].astype(F32) * slope + offset
                     values.append(value.astype(BF16))
                     target[k, group, lanes] = values[-1]
                 groups.append(jnp.concatenate(values, axis=1))

time: 80.9 us -> 80.9 us (level)
  no operation moved by 1% of the time
where the time goes in v8:
time: 80.9 us; the launch traced here: 79.4 us
  blocking collectives  46.8 us (58%)
  Pallas kernels  14.8 us (18%)
  waiting for transfers between devices  9.59 us (12%)
  starting transfers between devices  7.53 us (9%)
    all_to_all x1, blocking collectives, on_device(): lax.all_to_all(copies, 'dp', 0, 0, tiled=True, axis_index_groups=groups)  28.7 us
    all_to_all x1, blocking collectives, on_device(): lax.all_to_all(payload, 'dp', 0, 0, tiled=True, axis_index_groups=groups)  18.1 us
    ppermute x1, waiting for transfers between devices, on_device(): lax.ppermute(moved, 'section', [(i, i - 1) for i in range(1, sections)])  7.71 us
    pallas_call x1, Pallas kernels, on_device(): pl.pallas_call(second_kernel, out_shape=(shape((rank, tokens), F32), shap...  6.59 us
    pallas_call x1, Pallas kernels, on_device(): pl.pallas_call(first_kernel, out_shape=(shape((tokens, features), BF16),...  3.42 us
    ppermute x1, starting transfers between devices, on_device(): lax.ppermute(moved, 'section', [(i, i - 1) for i in range(1, sections)])  3.26 us
    ppermute x1, starting transfers between devices, on_device(): other = lax.ppermute(send, 'dp', others)  2.36 us
    pallas_call x1, Pallas kernels, on_device(): pl.pallas_call(lambda *refs: post_kernel(factor, *refs), out_shape=(shape...  2.34 us
  transfers between devices with their start and end apart: 3, of which 3 were waited for; matrix products, arithmetic and copies ran while one was open for 0% of the time, Pallas kernels for 5%

profile of v8, /device:TPU:56, one launch (start us, length us, event | category | flops | bytes accessed | tf_op | source)
XLA Modules:
  0.0 79.4 jit_solution(633156466411876118)
XLA Ops:
  0.6 1.1 %shard_map.84 = bf16[8,136,768]{2,1,0:T(8,128)(2,1)S(1)} custom-call(bf16[64,128]{1,0:T(8,128)(2,1)} %bitcast.17, bf16[64,768]{1,0:T(8,128)(2,1)} %bitcast.20, bf16[64,768]{1,0:T(8,128)(2,1)} %bitcast.21), custom_call_target="tpu_custom_call" | custom-call | tf_op jit(solution)/shard_map/pallas_call | solution.py:395
  1.7 0.0 copy-start
  1.7 0.0 copy-start.1
  1.7 28.7 %all_to_all.10.mine = bf16[8,136,768]{2,1,0:T(8,128)(2,1)S(1)} all-to-all(bf16[8,136,768]{2,1,0:T(8,128)(2,1)S(1)} %shard_map.84), channel_id=1, replica_groups={{0,2,4,6,8,10,12,14},{1,3,5,7,9,11,13,15},{16,18,20,22,24,26,28,30},{17..., dimensions={0} | all-to-all | bytes 3342336 | tf_op jit(solution)/shard_map/all_to_all | solution.py:403
  30.4 1.9 %collective-permute-start = (bf16[8,136,768]{2,1,0:T(8,128)(2,1)S(1)}, bf16[8,136,768]{2,1,0:T(8,128)(2,1)S(1)}, u32[]{:S(2)}, u32[]{:S(2)}) collective-permute-start(bf16[8,136,768]{2,1,0:T(8,128)(2,1)S(1)} %all_to_all.10.mine), channel_id=1, source_target_pairs={{0,1},{1,0},{2,3},{3,2},{4,5},{5,4},{6,7},{7,6},{8,9},{9,8},{10,11... | collective-permute-start | bytes 5013512 | tf_op jit(solution)/shard_map/ppermute | solution.py:404
  32.3 0.0 copy-done
  32.3 0.0 copy-done.1
  32.3 3.4 %shard_map.85 = (bf16[128,12288]{1,0:T(8,128)(2,1)S(1)}, bf16[128,64]{1,0:T(8,128)(2,1)S(1)}, f32[4,128,128]{2,1,0:T(8,128)S(1)}, f32[8,128,768]{2,1,0:T(8,128)S(1)}, f32[8,8,768]{2,1,0:T(8,128)S(1)}) custom-call(s32[1]{0:T(128)} %bitcast.parity, bf16[128,12288]{1,0:T(8,128)(2,1)} %bitcast.19, f32[1,12288]{1,0:T(1,128)S(1)} %copy-done, ...), custom_call_target="tpu_custom_call" | custom-call | bytes 25165824 | tf_op jit(solution)/shard_map/pallas_call | solution.py:406
  35.8 0.1 collective-permute-done.theirs
  35.8 6.6 %shard_map.86 = (f32[64,128]{1,0:T(8,128)S(1)}, bf16[8,128,768]{2,1,0:T(8,128)(2,1)S(1)}, f32[8,768]{1,0:T(8,128)S(1)}, bf16[8,80,768]{2,1,0:T(8,128)(2,1)S(1)}) custom-call(s32[1]{0:T(128)} %bitcast.parity, bf16[128,12288]{1,0:T(8,128)(2,1)S(1)} %get-tuple-element.20.x, f32[1,12288]{1,0:T(1,128)S(1)} %copy-done, ...), custom_call_target="tpu_custom_call" | custom-call | tf_op jit(solution)/shard_map/pallas_call | solution.py:421
  42.4 2.4 %collective-permute-start.1 = (bf16[8,80,768]{2,1,0:T(8,128)(2,1)S(1)}, bf16[8,80,768]{2,1,0:T(8,128)(2,1)S(1)}, u32[]{:S(2)}, u32[]{:S(2)}) collective-permute-start(bf16[8,80,768]{2,1,0:T(8,128)(2,1)S(1)} %get-tuple-element.28), channel_id=1, source_target_pairs={{0,1},{1,0},{2,3},{3,2},{4,5},{5,4},{6,7},{7,6},{8,9},{9,8},{10,11... | collective-permute-start | bytes 2949128 | tf_op jit(solution)/shard_map/ppermute | solution.py:441
  44.8 0.4 shard_map.87.keep
  45.2 1.8 %collective-permute-done.1.other = bf16[8,80,768]{2,1,0:T(8,128)(2,1)S(1)} collective-permute-done((bf16[8,80,768]{2,1,0:T(8,128)(2,1)S(1)}, bf16[8,80,768]{2,1,0:T(8,128)(2,1)S(1)}, u32[]{:S(2)}, u32[]{:S(2)}) %collective-permute-start.1) | collective-permute-done | bytes 983072 | tf_op jit(solution)/shard_map/ppermute | solution.py:441
  47.0 0.3 shard_map.88
  47.3 18.1 %all_to_all.11.refs_0_ = bf16[8,80,768]{2,1,0:T(8,128)(2,1)S(1)} all-to-all(bf16[8,80,768]{2,1,0:T(8,128)(2,1)S(1)} %shard_map.88), channel_id=1, replica_groups={{0,2,4,6,8,10,12,14},{1,3,5,7,9,11,13,15},{16,18,20,22,24,26,28,30},{17..., dimensions={0} | all-to-all | bytes 1966080 | tf_op jit(solution)/shard_map/all_to_all | solution.py:458
  65.4 2.3 %shard_map.89 = (f32[1,768]{1,0:T(1,128)S(1)}, f32[1,768]{1,0:T(1,128)S(1)}, bf16[64,896]{1,0:T(8,128)(2,1)S(1)}) custom-call(bf16[8,80,768]{2,1,0:T(8,128)(2,1)S(1)} %all_to_all.11.refs_0_, f32[64,128]{1,0:T(8,128)S(1)} %get-tuple-element.24.power_t.refs_1_), custom_call_target="tpu_custom_call" | custom-call | tf_op jit(solution)/shard_map/pallas_call | solution.py:461
  67.7 3.3 %collective-permute-start.2 = (bf16[64,896]{1,0:T(8,128)(2,1)S(1)}, bf16[64,896]{1,0:T(8,128)(2,1)S(1)}, u32[]{:S(2)}, u32[]{:S(2)}) collective-permute-start(bf16[64,896]{1,0:T(8,128)(2,1)S(1)} %get-tuple-element.29), channel_id=1, source_target_pairs={{16,0},{32,16},{48,32},{64,48},{80,64},{96,80},{112,96},{128,112},... | collective-permute-start | bytes 344072 | tf_op jit(solution)/shard_map/ppermute | solution.py:470
  71.0 7.7 %collective-permute-done.2.moved = bf16[64,896]{1,0:T(8,128)(2,1)S(1)} collective-permute-done((bf16[64,896]{1,0:T(8,128)(2,1)S(1)}, bf16[64,896]{1,0:T(8,128)(2,1)S(1)}, u32[]{:S(2)}, u32[]{:S(2)}) %collective-permute-start.2) | collective-permute-done | bytes 114720 | tf_op jit(solution)/shard_map/ppermute | solution.py:470
  78.7 0.7 shard_map.90
Async XLA Ops:
  1.7 30.6 %copy-start = (f32[1,12288]{1,0:T(1,128)S(1)}, f32[1,12288]{1,0:T(1,128)}, u32[]{:S(2)}) copy-start(f32[1,12288]{1,0:T(1,128)} %gain.3) | copy-start | bytes 147460
  1.7 30.6 %copy-start.1 = (bf16[1,128,64]{1,2,0:T(8,128)(2,1)S(1)}, bf16[1,128,64]{1,2,0:T(8,128)(2,1)}, u32[]{:S(2)}) copy-start(bf16[1,128,64]{1,2,0:T(8,128)(2,1)} %param.7) | copy-start | bytes 49156
  30.4 5.4 %collective-permute-start = (bf16[8,136,768]{2,1,0:T(8,128)(2,1)S(1)}, bf16[8,136,768]{2,1,0:T(8,128)(2,1)S(1)}, u32[]{:S(2)}, u32[]{:S(2)}) collective-permute-start(bf16[8,136,768]{2,1,0:T(8,128)(2,1)S(1)} %all_to_all.10.mine), channel_id=1, source_target_pairs={{0,1},{1,0},{2,3},{3,2},{4,5},{5,4},{6,7},{7,6},{8,9},{9,8},{10,11... | collective-permute-start | bytes 5013512 | tf_op jit(solution)/shard_map/ppermute | solution.py:404
  42.4 4.5 %collective-permute-start.1 = (bf16[8,80,768]{2,1,0:T(8,128)(2,1)S(1)}, bf16[8,80,768]{2,1,0:T(8,128)(2,1)S(1)}, u32[]{:S(2)}, u32[]{:S(2)}) collective-permute-start(bf16[8,80,768]{2,1,0:T(8,128)(2,1)S(1)} %get-tuple-element.28), channel_id=1, source_target_pairs={{0,1},{1,0},{2,3},{3,2},{4,5},{5,4},{6,7},{7,6},{8,9},{9,8},{10,11... | collective-permute-start | bytes 2949128 | tf_op jit(solution)/shard_map/ppermute | solution.py:441
  67.7 11.0 %collective-permute-start.2 = (bf16[64,896]{1,0:T(8,128)(2,1)S(1)}, bf16[64,896]{1,0:T(8,128)(2,1)S(1)}, u32[]{:S(2)}, u32[]{:S(2)}) collective-permute-start(bf16[64,896]{1,0:T(8,128)(2,1)S(1)} %get-tuple-element.29), channel_id=1, source_target_pairs={{16,0},{32,16},{48,32},{64,48},{80,64},{96,80},{112,96},{128,112},... | collective-permute-start | bytes 344072 | tf_op jit(solution)/shard_map/ppermute | solution.py:470

commit v9 on v8

--- a/solution.py
+++ b/solution.py
@@ -182,7 +182,8 @@
         gain_pass(2 * k + (1 - parity[0]), k, left, theirs, x, gain, rows, rebuilt, sums)
     mixed = totals[0] - totals[1] * (totals[2] * (1.0 / features))
     spread = unpack(totals[3][0:4] + totals[3][4:8], square) * (1.0 / (2 * half * tokens))
-    near = lax.dot_general(jnp.dot(mixed, spread, **EXACT), mixed, NT, **EXACT)
+    good = dict(precision=lax.Precision.HIGH, preferred_element_type=F32)
+    near = lax.dot_general(jnp.dot(mixed, spread, **good), mixed, NT, **good)
     row = lax.broadcasted_iota(jnp.int32, near.shape, 0)
     col = lax.broadcasted_iota(jnp.int32, near.shape, 1)
     level = jnp.sum(jnp.where(row == col, near, 0.0)) * 1e-05 + 1e-08

time: 80.9 us -> 80.8 us (level)
  no operation moved by 1% of the time
where the time goes in v9:
time: 80.8 us; the launch traced here: 79.4 us
  blocking collectives  46.8 us (58%)
  Pallas kernels  14.7 us (18%)
  waiting for transfers between devices  9.59 us (12%)
  starting transfers between devices  7.55 us (9%)
    all_to_all x1, blocking collectives, on_device(): lax.all_to_all(copies, 'dp', 0, 0, tiled=True, axis_index_groups=groups)  28.7 us
    all_to_all x1, blocking collectives, on_device(): lax.all_to_all(payload, 'dp', 0, 0, tiled=True, axis_index_groups=groups)  18.1 us
    ppermute x1, waiting for transfers between devices, on_device(): lax.ppermute(moved, 'section', [(i, i - 1) for i in range(1, sections)])  7.72 us
    pallas_call x1, Pallas kernels, on_device(): pl.pallas_call(second_kernel, out_shape=(shape((rank, tokens), F32), shap...  6.53 us
    pallas_call x1, Pallas kernels, on_device(): pl.pallas_call(first_kernel, out_shape=(shape((tokens, features), BF16),...  3.42 us
    ppermute x1, starting transfers between devices, on_device(): lax.ppermute(moved, 'section', [(i, i - 1) for i in range(1, sections)])  3.26 us
    ppermute x1, starting transfers between devices, on_device(): other = lax.ppermute(send, 'dp', others)  2.39 us
    pallas_call x1, Pallas kernels, on_device(): pl.pallas_call(lambda *refs: post_kernel(factor, *refs), out_shape=(shape...  2.35 us
  transfers between devices with their start and end apart: 3, of which 3 were waited for; matrix products, arithmetic and copies ran while one was open for 0% of the time, Pallas kernels for 5%

profile of v9, /device:TPU:56, one launch (start us, length us, event | category | flops | bytes accessed | tf_op | source)
XLA Modules:
  0.0 79.4 jit_solution(11872467947928084513)
XLA Ops:
  0.6 1.1 %shard_map.84 = bf16[8,136,768]{2,1,0:T(8,128)(2,1)S(1)} custom-call(bf16[64,128]{1,0:T(8,128)(2,1)} %bitcast.17, bf16[64,768]{1,0:T(8,128)(2,1)} %bitcast.20, bf16[64,768]{1,0:T(8,128)(2,1)} %bitcast.21), custom_call_target="tpu_custom_call" | custom-call | tf_op jit(solution)/shard_map/pallas_call | solution.py:396
  1.7 0.0 copy-start
  1.7 0.0 copy-start.1
  1.7 28.7 %all_to_all.10.mine = bf16[8,136,768]{2,1,0:T(8,128)(2,1)S(1)} all-to-all(bf16[8,136,768]{2,1,0:T(8,128)(2,1)S(1)} %shard_map.84), channel_id=1, replica_groups={{0,2,4,6,8,10,12,14},{1,3,5,7,9,11,13,15},{16,18,20,22,24,26,28,30},{17..., dimensions={0} | all-to-all | bytes 3342336 | tf_op jit(solution)/shard_map/all_to_all | solution.py:404
  30.4 1.9 %collective-permute-start = (bf16[8,136,768]{2,1,0:T(8,128)(2,1)S(1)}, bf16[8,136,768]{2,1,0:T(8,128)(2,1)S(1)}, u32[]{:S(2)}, u32[]{:S(2)}) collective-permute-start(bf16[8,136,768]{2,1,0:T(8,128)(2,1)S(1)} %all_to_all.10.mine), channel_id=1, source_target_pairs={{0,1},{1,0},{2,3},{3,2},{4,5},{5,4},{6,7},{7,6},{8,9},{9,8},{10,11... | collective-permute-start | bytes 5013512 | tf_op jit(solution)/shard_map/ppermute | solution.py:405
  32.3 0.0 copy-done
  32.3 0.0 copy-done.1
  32.3 3.4 %shard_map.85 = (bf16[128,12288]{1,0:T(8,128)(2,1)S(1)}, bf16[128,64]{1,0:T(8,128)(2,1)S(1)}, f32[4,128,128]{2,1,0:T(8,128)S(1)}, f32[8,128,768]{2,1,0:T(8,128)S(1)}, f32[8,8,768]{2,1,0:T(8,128)S(1)}) custom-call(s32[1]{0:T(128)} %bitcast.parity, bf16[128,12288]{1,0:T(8,128)(2,1)} %bitcast.19, f32[1,12288]{1,0:T(1,128)S(1)} %copy-done, ...), custom_call_target="tpu_custom_call" | custom-call | bytes 25165824 | tf_op jit(solution)/shard_map/pallas_call | solution.py:407
  35.8 0.1 collective-permute-done.theirs
  35.8 6.5 %shard_map.86 = (f32[64,128]{1,0:T(8,128)S(1)}, bf16[8,128,768]{2,1,0:T(8,128)(2,1)S(1)}, f32[8,768]{1,0:T(8,128)S(1)}, bf16[8,80,768]{2,1,0:T(8,128)(2,1)S(1)}) custom-call(s32[1]{0:T(128)} %bitcast.parity, bf16[128,12288]{1,0:T(8,128)(2,1)S(1)} %get-tuple-element.20.x, f32[1,12288]{1,0:T(1,128)S(1)} %copy-done, ...), custom_call_target="tpu_custom_call" | custom-call | tf_op jit(solution)/shard_map/pallas_call | solution.py:422
  42.4 2.4 %collective-permute-start.1 = (bf16[8,80,768]{2,1,0:T(8,128)(2,1)S(1)}, bf16[8,80,768]{2,1,0:T(8,128)(2,1)S(1)}, u32[]{:S(2)}, u32[]{:S(2)}) collective-permute-start(bf16[8,80,768]{2,1,0:T(8,128)(2,1)S(1)} %get-tuple-element.28), channel_id=1, source_target_pairs={{0,1},{1,0},{2,3},{3,2},{4,5},{5,4},{6,7},{7,6},{8,9},{9,8},{10,11... | collective-permute-start | bytes 2949128 | tf_op jit(solution)/shard_map/ppermute | solution.py:442
  44.8 0.4 shard_map.87.keep
  45.1 1.8 %collective-permute-done.1.other = bf16[8,80,768]{2,1,0:T(8,128)(2,1)S(1)} collective-permute-done((bf16[8,80,768]{2,1,0:T(8,128)(2,1)S(1)}, bf16[8,80,768]{2,1,0:T(8,128)(2,1)S(1)}, u32[]{:S(2)}, u32[]{:S(2)}) %collective-permute-start.1) | collective-permute-done | bytes 983072 | tf_op jit(solution)/shard_map/ppermute | solution.py:442
  46.9 0.3 shard_map.88
  47.2 18.1 %all_to_all.11.refs_0_ = bf16[8,80,768]{2,1,0:T(8,128)(2,1)S(1)} all-to-all(bf16[8,80,768]{2,1,0:T(8,128)(2,1)S(1)} %shard_map.88), channel_id=1, replica_groups={{0,2,4,6,8,10,12,14},{1,3,5,7,9,11,13,15},{16,18,20,22,24,26,28,30},{17..., dimensions={0} | all-to-all | bytes 1966080 | tf_op jit(solution)/shard_map/all_to_all | solution.py:459
  65.4 2.3 %shard_map.89 = (f32[1,768]{1,0:T(1,128)S(1)}, f32[1,768]{1,0:T(1,128)S(1)}, bf16[64,896]{1,0:T(8,128)(2,1)S(1)}) custom-call(bf16[8,80,768]{2,1,0:T(8,128)(2,1)S(1)} %all_to_all.11.refs_0_, f32[64,128]{1,0:T(8,128)S(1)} %get-tuple-element.24.power_t.refs_1_), custom_call_target="tpu_custom_call" | custom-call | tf_op jit(solution)/shard_map/pallas_call | solution.py:462
  67.7 3.3 %collective-permute-start.2 = (bf16[64,896]{1,0:T(8,128)(2,1)S(1)}, bf16[64,896]{1,0:T(8,128)(2,1)S(1)}, u32[]{:S(2)}, u32[]{:S(2)}) collective-permute-start(bf16[64,896]{1,0:T(8,128)(2,1)S(1)} %get-tuple-element.29), channel_id=1, source_target_pairs={{16,0},{32,16},{48,32},{64,48},{80,64},{96,80},{112,96},{128,112},... | collective-permute-start | bytes 344072 | tf_op jit(solution)/shard_map/ppermute | solution.py:471
  71.0 7.7 %collective-permute-done.2.moved = bf16[64,896]{1,0:T(8,128)(2,1)S(1)} collective-permute-done((bf16[64,896]{1,0:T(8,128)(2,1)S(1)}, bf16[64,896]{1,0:T(8,128)(2,1)S(1)}, u32[]{:S(2)}, u32[]{:S(2)}) %collective-permute-start.2) | collective-permute-done | bytes 114720 | tf_op jit(solution)/shard_map/ppermute | solution.py:471
  78.7 0.7 shard_map.90
Async XLA Ops:
  1.7 30.6 %copy-start = (f32[1,12288]{1,0:T(1,128)S(1)}, f32[1,12288]{1,0:T(1,128)}, u32[]{:S(2)}) copy-start(f32[1,12288]{1,0:T(1,128)} %gain.3) | copy-start | bytes 147460
  1.7 30.6 %copy-start.1 = (bf16[1,128,64]{1,2,0:T(8,128)(2,1)S(1)}, bf16[1,128,64]{1,2,0:T(8,128)(2,1)}, u32[]{:S(2)}) copy-start(bf16[1,128,64]{1,2,0:T(8,128)(2,1)} %param.7) | copy-start | bytes 49156
  30.4 5.4 %collective-permute-start = (bf16[8,136,768]{2,1,0:T(8,128)(2,1)S(1)}, bf16[8,136,768]{2,1,0:T(8,128)(2,1)S(1)}, u32[]{:S(2)}, u32[]{:S(2)}) collective-permute-start(bf16[8,136,768]{2,1,0:T(8,128)(2,1)S(1)} %all_to_all.10.mine), channel_id=1, source_target_pairs={{0,1},{1,0},{2,3},{3,2},{4,5},{5,4},{6,7},{7,6},{8,9},{9,8},{10,11... | collective-permute-start | bytes 5013512 | tf_op jit(solution)/shard_map/ppermute | solution.py:405
  42.4 4.6 %collective-permute-start.1 = (bf16[8,80,768]{2,1,0:T(8,128)(2,1)S(1)}, bf16[8,80,768]{2,1,0:T(8,128)(2,1)S(1)}, u32[]{:S(2)}, u32[]{:S(2)}) collective-permute-start(bf16[8,80,768]{2,1,0:T(8,128)(2,1)S(1)} %get-tuple-element.28), channel_id=1, source_target_pairs={{0,1},{1,0},{2,3},{3,2},{4,5},{5,4},{6,7},{7,6},{8,9},{9,8},{10,11... | collective-permute-start | bytes 2949128 | tf_op jit(solution)/shard_map/ppermute | solution.py:442
  67.7 11.0 %collective-permute-start.2 = (bf16[64,896]{1,0:T(8,128)(2,1)S(1)}, bf16[64,896]{1,0:T(8,128)(2,1)S(1)}, u32[]{:S(2)}, u32[]{:S(2)}) collective-permute-start(bf16[64,896]{1,0:T(8,128)(2,1)S(1)} %get-tuple-element.29), channel_id=1, source_target_pairs={{16,0},{32,16},{48,32},{64,48},{80,64},{96,80},{112,96},{128,112},... | collective-permute-start | bytes 344072 | tf_op jit(solution)/shard_map/ppermute | solution.py:471
